TPU v7x, 32 devices: a whole 2x2x4 slice. The times are simulated.
32 devices in a mesh: tower: 2 (over core), dp: 16 (over z, y, x).
Axes of the slice: x: 2, y: 2, z: 4, core: 2. Of those that a mesh axis runs over, the one named last changes fastest.
Arguments:
- picture_layer_entry: bfloat16 [768, 50, 768], P('dp'), may hold values from -6 to 6
- caption_layer_entry: bfloat16 [768, 16, 768], P('dp'), may hold values from -6 to 6
- usable_match_tallies: int32 [16], P('dp'), may hold values from 1 to 48, 576 in all
- similarity_exponent_factor: float32 [1], replicated, may hold values from 3.6 to 4.2
- picture_standardize_factors: bfloat16 [2, 768], replicated, may hold values from 0.5 to 1.5
- picture_layer_offsets: bfloat16 [6, 768], replicated, may hold values from -0.59765625 to 0.59765625
- picture_inner_offset: bfloat16 [3072], replicated, may hold values from -1.1953125 to 1.1953125
- picture_attend_entry_matrix: bfloat16 [768, 2304], replicated, may hold values from -0.21875 to 0.21875
- picture_attend_exit_matrix: bfloat16 [768, 768], replicated, may hold values from -1.5 to 1.5
- picture_widening_matrix: bfloat16 [768, 3072], replicated, may hold values from -0.21875 to 0.21875
- picture_narrowing_matrix: bfloat16 [3072, 768], replicated, may hold values from -0.109375 to 0.109375
- caption_standardize_factors: bfloat16 [2, 768], replicated, may hold values from 0.5 to 1.5
- caption_layer_offsets: bfloat16 [6, 768], replicated, may hold values from -0.59765625 to 0.59765625
- caption_inner_offset: bfloat16 [3072], replicated, may hold values from -1.1953125 to 1.1953125
- caption_attend_entry_matrix: bfloat16 [768, 2304], replicated, may hold values from -0.21875 to 0.21875
- caption_attend_exit_matrix: bfloat16 [768, 768], replicated, may hold values from -0.875 to 0.875
- caption_widening_matrix: bfloat16 [768, 3072], replicated, may hold values from -0.21875 to 0.21875
- caption_narrowing_matrix: bfloat16 [3072, 768], replicated, may hold values from -0.109375 to 0.109375
Outputs:
- loss: float32 [1], replicated
- exponent_derivative: float32 [1], replicated
- grad_tokens: float32 [768, 16, 768], P('dp', 'tower')
- grad_gains: float32 [2, 768], P('tower', 'dp')
- grad_biases: float32 [6, 768], P('tower', 'dp')
- grad_hidbias: float32 [3072], P(('tower', 'dp'))
- grad_qkv: float32 [768, 2304], P('dp', 'tower')
- grad_project: float32 [768, 768], P('dp', 'tower')
- grad_expand: float32 [768, 3072], P('dp', 'tower')
- grad_reduce: float32 [3072, 768], P(('tower', 'dp'))
Inputs may be any that keep to these rules, and one draw needn't show every extreme that they name: Index d of dp holds usable_match_tallies[d] valid pairs in its first slots of 48; the others are padding.
All inputs are finite; a program needn't handle non-finite values. No bound on the sum of `usable_match_tallies` on one device may be relied on, other than what follows from the above.
Results may differ from a plain program's by a relative error of at most 0.01.
The roundings to bfloat16 on the way count: a program that leaves them out, or rounds other values in their place, can miss the bound.
Values may be sent and summed in bfloat16 or wider, within the bound.
No kernel may reach another device: no remote copies, remote signals or barrier semaphores. Data moves between devices by JAX's collectives and lax.ppermute only.
A program may use at most 192 MiB of HBM per device.

v0:
```python
from functools import partial

import jax
import jax.numpy as jnp
from jax import lax
from jax.sharding import PartitionSpec as P

HEAD_DIM = 64


norm_eps = 1e-06
embed_eps = 1e-06


def from_partner(shard, axis, apart):
    return lax.ppermute(shard, axis, [(i, i ^ 1 << apart) for i in range(lax.axis_size(axis))])


def broadcast(block, axis, owner):
    block = jnp.where(lax.axis_index(axis) == owner, block, jnp.zeros_like(block))
    return lax.psum(block, axis)


def layer_norm(hidden, gain, shift):
    row_mean = jnp.mean(hidden, axis=-1, keepdims=True)
    centered = hidden - row_mean
    variance = jnp.mean(centered * centered, axis=-1, keepdims=True)
    return centered * lax.rsqrt(variance + norm_eps) * gain + shift


def embed_rows(output):
    pooled = jnp.mean(output, axis=1)
    return pooled * lax.rsqrt(jnp.sum(pooled * pooled, axis=-1, keepdims=True) + embed_eps)


def block_forward(hidden, gain_rows, biases, hidbias, w_qkv, w_proj, w_expand, w_reduce):
    batch_size, length, features = hidden.shape
    head_count = features // HEAD_DIM
    gain_f = gain_rows.astype(jnp.float32)
    bias_f = biases.astype(jnp.float32)
    normed = layer_norm(hidden, gain_f[0], bias_f[0]).astype(jnp.bfloat16)
    qkv_bias = jnp.concatenate([bias_f[2], jnp.zeros_like(bias_f[2]), bias_f[3]])
    qkv_all = (
        jnp.einsum("bsd,de->bse", normed, w_qkv, preferred_element_type=jnp.float32) + qkv_bias
    ).astype(jnp.bfloat16)
    qkv_split = qkv_all.reshape(batch_size, length, 3, head_count, HEAD_DIM)
    scores = jnp.einsum(
        "bqhe,bkhe->bhqk",
        qkv_split[:, :, 0],
        qkv_split[:, :, 1],
        preferred_element_type=jnp.float32,
    ) * HEAD_DIM ** (-0.5)
    attn_probs = jax.nn.softmax(scores, axis=-1)
    probs_low = attn_probs.astype(jnp.bfloat16)
    mixed_out = (
        jnp.einsum(
            "bhqk,bkhe->bqhe", probs_low, qkv_split[:, :, 2], preferred_element_type=jnp.float32
        )
        .astype(jnp.bfloat16)
        .reshape(batch_size, length, features)
    )
    attended = (
        jnp.einsum("bsd,de->bse", mixed_out, w_proj, preferred_element_type=jnp.float32) + bias_f[4]
    )
    middle = hidden + attended
    normed_two = layer_norm(middle, gain_f[1], bias_f[1]).astype(jnp.bfloat16)
    inner_pre = jnp.einsum(
        "bsd,df->bsf", normed_two, w_expand, preferred_element_type=jnp.float32
    ) + hidbias.astype(jnp.float32)
    active = jax.nn.gelu(inner_pre, approximate=False).astype(jnp.bfloat16)
    branch = (
        jnp.einsum("bsf,fd->bsd", active, w_reduce, preferred_element_type=jnp.float32) + bias_f[5]
    )
    return (
        middle + branch,
        (
            normed,
            qkv_split,
            attn_probs,
            probs_low,
            mixed_out,
            middle,
            normed_two,
            inner_pre,
            active,
        ),
    )


def block_backward(
    grad_out, hidden, kept_state, gain_rows, biases, hidbias, w_qkv, w_proj, w_expand, w_reduce
):
    normed, qkv_split, attn_probs, probs_low, mixed_out, middle, normed_two, inner_pre, active = (
        kept_state
    )
    batch_size, length, features = hidden.shape
    head_count = features // HEAD_DIM
    gain_f = gain_rows.astype(jnp.float32)
    bias_f = biases.astype(jnp.float32)
    grad_branch = grad_out.astype(jnp.bfloat16)
    grad_reduce = jnp.einsum("bsf,bsd->fd", active, grad_branch, preferred_element_type=jnp.float32)
    grad_rbias = jnp.sum(grad_branch, axis=(0, 1), dtype=jnp.float32)
    grad_active = jnp.einsum(
        "bsd,fd->bsf", grad_branch, w_reduce, preferred_element_type=jnp.float32
    )
    _, gelu_back = jax.vjp(partial(jax.nn.gelu, approximate=False), inner_pre)
    grad_inner = gelu_back(grad_active)[0].astype(jnp.bfloat16)
    grad_expand = jnp.einsum(
        "bsd,bsf->df", normed_two, grad_inner, preferred_element_type=jnp.float32
    )
    grad_hidbias = jnp.sum(grad_inner, axis=(0, 1), dtype=jnp.float32)
    grad_normed_two = jnp.einsum(
        "bsf,df->bsd", grad_inner, w_expand, preferred_element_type=jnp.float32
    )
    _, norm_back_two = jax.vjp(layer_norm, middle, gain_f[1], bias_f[1])
    grad_mid_part, grad_gain_two, grad_shift_two = norm_back_two(grad_normed_two)
    grad_middle = grad_out + grad_mid_part
    grad_attended = grad_middle.astype(jnp.bfloat16)
    grad_project = jnp.einsum(
        "bsd,bse->de", mixed_out, grad_attended, preferred_element_type=jnp.float32
    )
    grad_pbias = jnp.sum(grad_attended, axis=(0, 1), dtype=jnp.float32)
    grad_mixed = (
        jnp.einsum("bse,de->bsd", grad_attended, w_proj, preferred_element_type=jnp.float32)
        .astype(jnp.bfloat16)
        .reshape(batch_size, length, head_count, HEAD_DIM)
    )
    queries = qkv_split[:, :, 0]
    key_part = qkv_split[:, :, 1]
    values = qkv_split[:, :, 2]
    grad_probs = jnp.einsum(
        "bqhe,bkhe->bhqk", grad_mixed, values, preferred_element_type=jnp.float32
    )
    grad_scores = (
        attn_probs * (grad_probs - jnp.sum(attn_probs * grad_probs, axis=-1, keepdims=True))
    ).astype(jnp.bfloat16)
    score_scale = HEAD_DIM ** (-0.5)
    grad_queries = (
        jnp.einsum("bhqk,bkhe->bqhe", grad_scores, key_part, preferred_element_type=jnp.float32)
        * score_scale
    )
    grad_keys = (
        jnp.einsum("bhqk,bqhe->bkhe", grad_scores, queries, preferred_element_type=jnp.float32)
        * score_scale
    )
    grad_values = jnp.einsum(
        "bhqk,bqhe->bkhe", probs_low, grad_mixed, preferred_element_type=jnp.float32
    )
    grad_qkv_all = (
        jnp.stack([grad_queries, grad_keys, grad_values], axis=2)
        .astype(jnp.bfloat16)
        .reshape(batch_size, length, 3 * features)
    )
    grad_qkv = jnp.einsum("bsd,bse->de", normed, grad_qkv_all, preferred_element_type=jnp.float32)
    qkv_sums = jnp.sum(grad_qkv_all, axis=(0, 1), dtype=jnp.float32)
    grad_normed = jnp.einsum("bse,de->bsd", grad_qkv_all, w_qkv, preferred_element_type=jnp.float32)
    _, norm_back_one = jax.vjp(layer_norm, hidden, gain_f[0], bias_f[0])
    grad_hid_part, grad_gain_one, grad_shift_one = norm_back_one(grad_normed)
    grad_hidden = grad_middle + grad_hid_part
    grad_gains = jnp.stack([grad_gain_one, grad_gain_two])
    grad_biases = jnp.stack(
        [
            grad_shift_one,
            grad_shift_two,
            qkv_sums[:features],
            qkv_sums[2 * features :],
            grad_pbias,
            grad_rbias,
        ]
    )
    return (
        grad_hidden,
        (grad_gains, grad_biases, grad_hidbias, grad_qkv, grad_project, grad_expand, grad_reduce),
    )


def column_halves(matrix, groups):
    rows, cols = matrix.shape
    blocks = matrix.reshape(groups, rows // groups, 2, cols // 2)
    return jnp.transpose(blocks, (2, 0, 1, 3)).reshape(2 * rows, cols // 2)


def arrange_grads(weight_grads, groups):
    gains_grad, biases_grad, hidbias_grad, qkv_grad, project_grad, expand_grad, reduce_grad = (
        weight_grads
    )
    width = gains_grad.shape[1] // groups
    gains_rows = gains_grad.reshape(2 * groups, width)
    biases_rows = jnp.transpose(biases_grad.reshape(2, 3, groups, width), (0, 2, 1, 3)).reshape(
        2 * groups, 3, width
    )
    return (
        gains_rows,
        biases_rows,
        hidbias_grad,
        column_halves(qkv_grad, groups),
        column_halves(project_grad, groups),
        column_halves(expand_grad, groups),
        reduce_grad,
    )


def body(
    picture_layer_entry,
    caption_layer_entry,
    usable_match_tallies,
    similarity_exponent_factor,
    picture_standardize_factors,
    picture_layer_offsets,
    picture_inner_offset,
    picture_attend_entry_matrix,
    picture_attend_exit_matrix,
    picture_widening_matrix,
    picture_narrowing_matrix,
    caption_standardize_factors,
    caption_layer_offsets,
    caption_inner_offset,
    caption_attend_entry_matrix,
    caption_attend_exit_matrix,
    caption_widening_matrix,
    caption_narrowing_matrix,
):
    tower_index = lax.axis_index("tower")
    is_text = tower_index == 1
    dp_index = lax.axis_index("dp")
    dp_count = lax.axis_size("dp")
    pair_rows = caption_layer_entry.shape[0]
    image_set = (
        picture_standardize_factors,
        picture_layer_offsets,
        picture_inner_offset,
        picture_attend_entry_matrix,
        picture_attend_exit_matrix,
        picture_widening_matrix,
        picture_narrowing_matrix,
    )
    caption_parameter_bundle = (
        caption_standardize_factors,
        caption_layer_offsets,
        caption_inner_offset,
        caption_attend_entry_matrix,
        caption_attend_exit_matrix,
        caption_widening_matrix,
        caption_narrowing_matrix,
    )

    def image_side():
        output, _ = block_forward(picture_layer_entry.astype(jnp.float32), *image_set)
        return embed_rows(output)

    def text_side():
        output, _ = block_forward(
            caption_layer_entry.astype(jnp.float32), *caption_parameter_bundle
        )
        return embed_rows(output)

    own_emb = lax.cond(is_text, text_side, image_side).astype(jnp.bfloat16)
    count_low = usable_match_tallies.astype(jnp.bfloat16)
    own_all, counts_all = (
        lax.all_gather(own_emb, "dp", axis=0, tiled=True),
        lax.all_gather(count_low, "dp", axis=0, tiled=True),
    )
    partner = from_partner(own_emb, "tower", 0)
    partner_all = lax.all_gather(partner, "dp", axis=0, tiled=True)
    text_own = jnp.where(is_text, own_emb, partner)
    image_own = jnp.where(is_text, partner, own_emb)
    texts_all = jnp.where(is_text, own_all, partner_all)
    images_all = jnp.where(is_text, partner_all, own_all)
    total_rows = texts_all.shape[0]
    slot_ids = jnp.arange(total_rows, dtype=jnp.int32)
    col_valid = (slot_ids % pair_rows).astype(jnp.float32) < jnp.repeat(
        counts_all.astype(jnp.float32), pair_rows
    )
    row_valid = (jnp.arange(pair_rows, dtype=jnp.int32) < usable_match_tallies[0]).astype(
        jnp.float32
    )
    similarity_multiplier = jnp.exp(similarity_exponent_factor[0])
    first_col = dp_index * pair_rows
    identity = jnp.eye(pair_rows, dtype=jnp.float32)

    def side_terms(own_rows, other_rows):
        raw_scores_matrix = similarity_multiplier * jnp.einsum(
            "oq,fq->of", own_rows, other_rows, preferred_element_type=jnp.float32
        )
        masked = jnp.where(col_valid[None, :], raw_scores_matrix, -1000000000.0)
        row_max = jnp.max(masked, axis=1, keepdims=True)
        exponent = jnp.exp(masked - row_max)
        row_total = jnp.sum(exponent, axis=1, keepdims=True)
        log_total = row_max[:, 0] + jnp.log(row_total[:, 0])
        diagonal = jnp.sum(
            lax.dynamic_slice_in_dim(raw_scores_matrix, first_col, pair_rows, 1) * identity, axis=1
        )
        loss_term = jnp.sum(row_valid * (log_total - diagonal))
        softened = exponent / row_total
        own_block = lax.dynamic_slice_in_dim(softened, first_col, pair_rows, 1) - identity
        softened = lax.dynamic_update_slice_in_dim(softened, own_block, first_col, 1)
        grad_soft = (0.5 * row_valid[:, None] * softened).astype(jnp.bfloat16)
        temp_term = jnp.sum(grad_soft * raw_scores_matrix)
        return (loss_term, grad_soft, temp_term, log_total)

    term_text, grad_text_side, temp_text, _ = side_terms(text_own, images_all)
    term_image, grad_image_side, temp_image, image_lse = side_terms(image_own, texts_all)
    derivative_here = similarity_multiplier * jnp.dot(
        grad_text_side, images_all, preferred_element_type=jnp.float32
    )
    grad_remote = lax.psum_scatter(
        similarity_multiplier
        * jnp.einsum("pn,pd->nd", grad_image_side, image_own, preferred_element_type=jnp.float32),
        "dp",
        scatter_dimension=0,
        tiled=True,
    )
    grad_embed = derivative_here + grad_remote
    loss_portion = 0.5 * jnp.where(is_text, term_text, term_image)
    warmth_portion = jnp.where(is_text, temp_text, temp_image)
    loss_accumulated, warmth_accumulated = lax.psum((loss_portion, warmth_portion), ("tower", "dp"))
    count_total = jnp.sum(counts_all.astype(jnp.float32))
    loss = (loss_accumulated / count_total).reshape(1)
    exponent_derivative = warmth_accumulated.reshape(1)

    def text_back():
        hidden = caption_layer_entry.astype(jnp.float32)
        output, kept_state = block_forward(hidden, *caption_parameter_bundle)
        _, embed_back = jax.vjp(embed_rows, output)
        grad_out = embed_back(grad_embed)[0]
        return block_backward(grad_out, hidden, kept_state, *caption_parameter_bundle)

    def blank_back():
        return (
            jnp.zeros(caption_layer_entry.shape, jnp.float32),
            jax.tree.map(
                lambda weight_arr: jnp.zeros(weight_arr.shape, jnp.float32),
                caption_parameter_bundle,
            ),
        )

    grad_hidden, weight_grads = lax.cond(is_text, text_back, blank_back)
    arranged = arrange_grads(weight_grads, dp_count)
    a_gains, a_biases, a_hidbias, a_qkv, a_project, a_expand, a_reduce = arranged
    shards = (
        lax.psum_scatter(a_gains, ("tower", "dp"), scatter_dimension=0, tiled=True),
        lax.psum_scatter(a_biases, ("tower", "dp"), scatter_dimension=0, tiled=True),
        lax.psum_scatter(a_hidbias, ("tower", "dp"), scatter_dimension=0, tiled=True),
        lax.psum_scatter(a_qkv, ("tower", "dp"), scatter_dimension=0, tiled=True),
        lax.psum_scatter(a_project, ("tower", "dp"), scatter_dimension=0, tiled=True),
        lax.psum_scatter(a_expand, ("tower", "dp"), scatter_dimension=0, tiled=True),
        lax.psum_scatter(a_reduce, ("tower", "dp"), scatter_dimension=0, tiled=True),
    )
    half_len = caption_layer_entry.shape[1] // 2
    shared_grad = broadcast(grad_hidden.astype(jnp.bfloat16), "tower", 1).astype(grad_hidden.dtype)
    grad_tokens = jnp.where(is_text, shared_grad[:, half_len:], shared_grad[:, :half_len])
    biases_shard = shards[1].reshape(3, shards[1].shape[-1])
    return (
        loss,
        exponent_derivative,
        grad_tokens,
        shards[0],
        biases_shard,
        shards[2],
        shards[3],
        shards[4],
        shards[5],
        shards[6],
    )


def solution(mesh):
    in_specs = (
        P("dp", None, None),
        P("dp", None, None),
        P("dp"),
        P(),
        P(),
        P(),
        P(),
        P(),
        P(),
        P(),
        P(),
        P(),
        P(),
        P(),
        P(),
        P(),
        P(),
        P(),
    )
    out_specs = (
        P(),
        P(),
        P("dp", "tower", None),
        P("tower", "dp"),
        P("tower", "dp"),
        P(("tower", "dp")),
        P("dp", "tower"),
        P("dp", "tower"),
        P("dp", "tower"),
        P(("tower", "dp"), None),
    )
    return jax.shard_map(body, mesh=mesh, in_specs=in_specs, out_specs=out_specs, check_vma=False)
```

profile of v0, /device:TPU:0, one launch (start us, length us, event | category | flops | bytes accessed | tf_op | source)
XLA Modules:
  0.0 1289.5 jit_solution(16902557255273559138)
XLA Ops:
  7.2 269.8 %conditional.7 = (bf16[48,768]{1,0:T(8,128)(2,1)S(1)}) conditional(s32[]{:T(128)} %convert_element_type.196, (bf16[48,50,768]{2,0,1:T(8,128)(2,1)}, bf16[2,768]{1,0:T(2,128)(2,1)}, bf16[6,768]{1,0:T(8,128)(2,1)}, bf16[768,2304]{1,0:T(8,128)(2,1)}, bf16[768,768]{1,0:T(8,128)(2,1)}, /*index=5*/bf16[768,3072]{1,0:T(8,128)(2,1)}, ...), branch_computations={%region_0.0_spmd, %region_9.0_spmd} | conditional | flops 34900582400 | bytes 248296160
  9.9 3.1 convert_reduce_fusion
  13.0 3.0 fusion.20
  16.1 14.5 %add_convert_fusion = bf16[48,50,2304]{2,1,0:T(8,128)(2,1)} fusion(f32[2304]{0:T(1024)S(1)} %pad_maximum_fusion, f32[768]{0:T(1024)S(1)} %get-tuple-element.169, f32[768]{0:T(1024)S(1)} %get-tuple-element.225, f32[48,50]{1,0:T(8,128)S(1)} %add_rsqrt_fusion.1, f32[48,50]{1,0:T(8,128)S(1)} %broadcast_multiply_fusion.2, bf16[768,2304]{1,0:T(8,128)(2,1)S(1)} %copy-done.83, ...), kind=kOutput, calls=%fused_computation.20 | convolution fusion | flops 8515584000 | bytes 18319104 | tf_op jit(solution)/shard_map/cond/branch_0_fun/bsd,de->bse/dot_general | solution.py:44
  30.6 27.8 %reshape.317 = bf16[48,50,3,12,64]{4,3,2,1,0:T(8,128)(2,1)} reshape(bf16[48,50,2304]{2,1,0:T(8,128)(2,1)} %add_convert_fusion) | data formatting | bytes 22118400 | tf_op jit(solution)/shard_map/cond/branch_0_fun/reshape | solution.py:46
  58.4 22.4 %fusion.264 = (bf16[48,50,1,12,64]{4,3,2,1,0:T(8,128)(2,1)}, bf16[48,50,1,12,64]{4,3,2,1,0:T(8,128)(2,1)}, bf16[48,50,1,12,64]{4,3,2,1,0:T(8,128)(2,1)}) fusion(bf16[48,50,3,12,64]{4,3,2,1,0:T(8,128)(2,1)} %reshape.317), kind=kLoop, calls=%fused_computation.399 | loop fusion | bytes 22118400 | tf_op jit(solution)/shard_map/cond/branch_0_fun/slice | solution.py:57
  80.8 14.4 %fusion.25 = f32[48,12,50,50]{2,3,1,0:T(8,128)} fusion(bf16[48,50,1,12,64]{4,3,2,1,0:T(8,128)(2,1)} %get-tuple-element.220, bf16[48,50,1,12,64]{4,3,2,1,0:T(8,128)(2,1)} %get-tuple-element.219), kind=kOutput, calls=%fused_computation.38 | convolution fusion | flops 184320000 | bytes 13132800 | tf_op jit(solution)/shard_map/cond/branch_0_fun/bqhe,bkhe->bhqk/dot_general | solution.py:47
  95.2 19.1 %fusion.265 = (f32[48,12,50]{2,1,0:T(8,128)S(1)}, f32[48,12,50,50]{2,3,1,0:T(8,128)}) fusion(f32[48,12,50,50]{2,3,1,0:T(8,128)} %fusion.25), kind=kOutput, calls=%fused_computation.400 | output fusion | flops 5760049 | bytes 11635200 | tf_op jit(solution)/shard_map/cond/branch_0_fun/sub | solution.py:53
  114.2 13.8 %convert_bitcast_fusion = bf16[48,50,12,64]{3,1,2,0:T(8,128)(2,1)} fusion(f32[48,12,50,50]{2,3,1,0:T(8,128)} %get-tuple-element.222, f32[48,12,50]{2,1,0:T(8,128)S(1)} %get-tuple-element.221, bf16[48,50,1,12,64]{4,3,2,1,0:T(8,128)(2,1)} %get-tuple-element.218), kind=kOutput, calls=%fused_computation.44 | convolution fusion | flops 189043200 | bytes 13248000 | tf_op jit(solution)/shard_map/cond/branch_0_fun/bhqk,bkhe->bqhe/dot_general | solution.py:56
  128.0 8.8 copy.154
  136.8 12.6 reshape.316
  149.4 8.3 fusion.266
  159.2 86.8 %fusion.294 = bf16[48,50,3072]{2,1,0:T(8,128)(2,1)} fusion(f32[3072]{0:T(1024)S(1)} %convert_element_type.145, bf16[768,3072]{1,0:T(8,128)(2,1)S(1)} %bitcast.183, f32[48,50,768]{2,1,0:T(8,128)S(1)} %get-tuple-element.224, f32[768]{0:T(1024)S(1)} %get-tuple-element.164, f32[768]{0:T(1024)S(1)} %get-tuple-element.226, ...), kind=kOutput, calls=%fused_computation.4.clone.clone.clone.clone.1 | convolution fusion | flops 11820441600 | bytes 26874624 | tf_op jit(solution)/shard_map/cond/branch_0_fun/bsd,df->bsf/dot_general | solution.py:67
  246.0 17.5 %add_reduce_fusion = f32[48,768]{1,0:T(8,128)S(1)} fusion(f32[48,50,768]{2,1,0:T(8,128)S(1)} %get-tuple-element.224, f32[768]{0:T(1024)S(1)} %copy-done.78, bf16[3072,768]{1,0:T(8,128)(2,1)} %get-tuple-element.126, bf16[48,50,3072]{2,1,0:T(8,128)(2,1)} %fusion.294), kind=kOutput, calls=%fused_computation.41 | convolution fusion | flops 11330113536 | bytes 26987520 | tf_op jit(solution)/shard_map/cond/branch_0_fun/bsf,fd->bsd/dot_general | solution.py:72
  282.6 43.7 %all-reduce = bf16[16]{0:T(256)(128)(2,1)S(1)} all-reduce(bf16[16]{0:T(256)(128)(2,1)S(1)} %dynamic-update-slice), channel_id=1, replica_groups=mesh['tower'=2,'dp'=16] {'dp'}, use_global_device_ids=true, to_apply=%add | all-reduce | flops 16 | bytes 64
  327.8 8.9 all-gather.5.cloned.1.call-done
  336.7 58.4 %all-gather.3.cloned.1.call-done = bf16[768,768]{1,0:T(8,128)(2,1)} async-done(((bf16[48,768]{1,0:T(8,128)(2,1)}), bf16[768,768]{1,0:T(8,128)(2,1)}) %all-gather.3.cloned.1.call-update) | async-done | bytes 1179664 | tf_op jit(solution)/shard_map/all_gather | solution.py:264
  404.4 2.9 convolution_multiply_fusion
  412.4 122.6 %reduce-scatter.6.cloned.1.call-done = f32[48,768]{1,0:T(8,128)} async-done(((f32[768,768]{1,0:T(8,128)}), f32[48,768]{1,0:T(8,128)}) %reduce-scatter.6.cloned.1.call-update) | async-done | bytes 147472 | tf_op jit(solution)/shard_map/reduce_scatter | solution.py:306
  534.9 23.1 %conditional.8 = (f32[2,768]{1,0:T(2,128)}, f32[6,768]{1,0:T(8,128)}, f32[3072]{0:T(1024)}, f32[768,2304]{1,0:T(8,128)}, f32[768,768]{1,0:T(8,128)}, /*index=5*/...) conditional(s32[]{:T(128)} %convert_element_type.196, () %tuple.36, ...), branch_computations={%region_32.33_spmd, %region_33.56_spmd} | conditional | flops 32992813056 | bytes 446656928 | solution.py:337
  536.8 3.4 broadcast.543
  541.7 4.8 broadcast.545
  546.5 4.3 broadcast.546
  563.8 9.3 reshape.289
  573.0 6.4 copy.147
  579.6 13.1 %reshape.293 = f32[16,48,2,1536]{3,2,1,0:T(2,128)} reshape(f32[768,3072]{1,0:T(8,128)} %get-tuple-element.109) | data formatting | bytes 18874368 | tf_op jit(solution)/shard_map/reshape | solution.py:179
  592.7 9.1 copy.149
  609.7 229.2 %all-reduce.4 = (f32[]{:T(128)}, f32[1]{0:T(128)}, f32[32,48]{1,0:T(8,128)S(1)}, f32[32,3,48]{2,1,0:T(4,128)S(1)}, f32[3072]{0:T(1024)S(1)}) all-reduce(f32[]{:T(128)S(6)} %mul.416, f32[1]{0:T(128)} %bitcast.38, f32[32,48]{1,0:T(8,128)S(1)} %reshape.285, ...), channel_id=1, replica_groups=mesh['tower'=2,'dp'=16] {'tower','dp'}, use_global_device_ids=true, to_apply=%region_26.27 | all-reduce | flops 9218 | bytes 73744 | tf_op jit(solution)/shard_map/psum | solution.py:316
  844.6 27.7 %reduce-scatter.10.cloned.1.call-done = f32[48,384]{1,0:T(8,128)} async-done(((f32[1536,384]{1,0:T(8,128)}), f32[48,384]{1,0:T(8,128)}) %reduce-scatter.10.cloned.1.call-update) | async-done | bytes 73744 | tf_op jit(solution)/shard_map/reduce_scatter | solution.py:345
  872.4 125.1 %reduce-scatter.8.cloned.1.call-done = f32[48,1152]{1,0:T(8,128)} async-done(((f32[1536,1152]{1,0:T(8,128)}), f32[48,1152]{1,0:T(8,128)}) %reduce-scatter.8.cloned.1.call-update) | async-done | bytes 221200 | tf_op jit(solution)/shard_map/reduce_scatter | solution.py:344
  997.5 141.5 %reduce-scatter.12.cloned.1.call-done = f32[48,1536]{1,0:T(8,128)} async-done(((f32[1536,1536]{1,0:T(8,128)}), f32[48,1536]{1,0:T(8,128)}) %reduce-scatter.12.cloned.1.call-update) | async-done | bytes 294928 | tf_op jit(solution)/shard_map/reduce_scatter | solution.py:346
  1138.9 142.1 %reduce-scatter.14.cloned.1.call-done = f32[96,768]{1,0:T(8,128)} async-done(((f32[3072,768]{1,0:T(8,128)}), f32[96,768]{1,0:T(8,128)}) %reduce-scatter.14.cloned.1.call-update) | async-done | bytes 294928 | tf_op jit(solution)/shard_map/reduce_scatter | solution.py:347
  (139 shorter events, 43.8 us)
Async XLA Ops:
  7.2 329.6 %all-gather.5.cloned.1.call-start = ((), (), s32[]{:S(2)}) async-start(), calls=%async_computation.6 | async-start | bytes 1253376 | tf_op jit(solution)/shard_map/all_gather | solution.py:260
  7.2 5.8 copy-start.9
  7.3 8.8 copy-start.83
  136.8 12.6 copy-start.84
  149.4 9.8 slice-start.4
  149.4 8.3 copy-start.68
  149.4 9.8 slice-start.5
  159.2 86.8 %copy-start.78 = (f32[768]{0:T(1024)S(1)}, f32[768]{0:T(1024)}, u32[]{:S(2)}) copy-start(f32[768]{0:T(1024)} %get-tuple-element.165) | copy-start | bytes 9220 | tf_op jit(solution)/shard_map/conditional.1
  277.7 117.5 %all-gather.3.cloned.1.call-start = ((), (), s32[]{:S(2)}) async-start(), calls=%async_computation.5 | async-start | bytes 1253376 | tf_op jit(solution)/shard_map/all_gather | solution.py:264
  277.7 1.5 collective-permute-start
  279.9 255.0 %reduce-scatter.6.cloned.1.call-start = ((), (), s32[]{:S(2)}) async-start(), calls=%async_computation.7 | async-start | bytes 2506752 | tf_op jit(solution)/shard_map/reduce_scatter | solution.py:306
  327.8 69.1 %copy-start.67 = (pred[768]{0:T(1024)(128)(4,1)}, pred[768]{0:T(1024)(128)(4,1)S(1)}, u32[]{:S(2)}) copy-start(pred[768]{0:T(1024)(128)(4,1)S(1)} %fusion.254) | copy-start | bytes 2308
  397.0 3.2 copy-start.18
  397.0 13.4 %copy-start.13 = (bf16[768,768]{1,0:T(8,128)(2,1)S(1)}, bf16[768,768]{1,0:T(8,128)(2,1)}, u32[]{:S(2)}) copy-start(bf16[768,768]{1,0:T(8,128)(2,1)} %all-gather.5.cloned.1.call-done) | copy-start | bytes 3538948
  397.0 13.4 %copy-start.14 = (bf16[768,768]{1,0:T(8,128)(2,1)S(1)}, bf16[768,768]{1,0:T(8,128)(2,1)}, u32[]{:S(2)}) copy-start(bf16[768,768]{1,0:T(8,128)(2,1)} %all-gather.3.cloned.1.call-done) | copy-start | bytes 3538948
  399.1 2.6 copy-start.35
  399.1 3.9 copy-start.69
  399.1 3.9 copy-start.73
  399.1 135.8 %copy-start = (bf16[48,16,768]{2,1,0:T(8,128)(2,1)S(1)}, bf16[48,16,768]{2,1,0:T(8,128)(2,1)}, u32[]{:S(2)}) copy-start(bf16[48,16,768]{2,1,0:T(8,128)(2,1)} %param.23) | copy-start | bytes 3538948
  399.1 135.8 %copy-start.62 = (bf16[6,768]{1,0:T(8,128)(2,1)S(1)}, bf16[6,768]{1,0:T(8,128)(2,1)}, u32[]{:S(2)}) copy-start(bf16[6,768]{1,0:T(8,128)(2,1)} %param.34) | copy-start | bytes 27652
  399.1 135.8 %copy-start.66 = (bf16[2,768]{1,0:T(2,128)(2,1)S(1)}, bf16[2,768]{1,0:T(2,128)(2,1)}, u32[]{:S(2)}) copy-start(bf16[2,768]{1,0:T(2,128)(2,1)} %param.33) | copy-start | bytes 9220
  400.1 2.8 copy-start.71
  400.2 2.8 copy-start.75
  407.4 434.5 %all-reduce.7.cloned.1.call-start = ((), (), s32[]{:S(2)}) async-start(), calls=%async_computation.8 | async-start | bytes 2359296 | tf_op jit(solution)/shard_map/psum | solution.py:21
  559.2 313.2 %reduce-scatter.10.cloned.1.call-start = ((), (), s32[]{:S(2)}) async-start(), calls=%async_computation.10 | async-start | bytes 2433024 | tf_op jit(solution)/shard_map/reduce_scatter | solution.py:345
  563.7 433.7 %reduce-scatter.8.cloned.1.call-start = ((), (), s32[]{:S(2)}) async-start(), calls=%async_computation.9 | async-start | bytes 7299072 | tf_op jit(solution)/shard_map/reduce_scatter | solution.py:344
  579.5 559.4 %reduce-scatter.12.cloned.1.call-start = ((), (), s32[]{:S(2)}) async-start(), calls=%async_computation.11 | async-start | bytes 9732096 | tf_op jit(solution)/shard_map/reduce_scatter | solution.py:346
  601.9 679.2 %reduce-scatter.14.cloned.1.call-start = ((), (), s32[]{:S(2)}) async-start(), calls=%async_computation.12 | async-start | bytes 9732096 | tf_op jit(solution)/shard_map/reduce_scatter | solution.py:347
  602.0 4.0 copy-start.34
  602.0 4.0 copy-start.36
  602.0 4.0 copy-start.38
  602.0 4.0 copy-start.77
  (11 other events, 14.7 us)
Sparse Core Ops, SparseCore 0:
  277.8 58.8 all-gather.4
  340.1 54.9 all-gather.2
  407.5 127.3 reduce-scatter.5
  559.3 206.9 all-reduce.6
  772.0 100.2 reduce-scatter.9
  879.4 117.9 reduce-scatter.7
  1003.9 134.9 reduce-scatter.11
  1146.4 134.6 reduce-scatter.13
where the time goes:
time: 1300 us; the launch traced here: 1290 us
  waiting for transfers between devices  628 us (48%)
  blocking collectives  273 us (21%)
  matrix products  164 us (13%)
  local copies, waits for them, and re-layouts  141 us (11%)
  other arithmetic  41.3 us (3%)
  between operations  21.4 us (2%)
  loops' own time  19.7 us (2%)
    psum x1, blocking collectives, body(): lax.psum((loss_portion, warmth_portion), ('tower', 'dp'))  229 us
    reduce_scatter x1, waiting for transfers between devices, body(): lax.psum_scatter(a_reduce, ('tower', 'dp'), scatter_dimension=0, tiled=True)  142 us
    reduce_scatter x1, waiting for transfers between devices, body(): lax.psum_scatter(a_expand, ('tower', 'dp'), scatter_dimension=0, tiled=True)  141 us
    reduce_scatter x1, waiting for transfers between devices, body(): lax.psum_scatter(a_qkv, ('tower', 'dp'), scatter_dimension=0, tiled=True)  125 us
    reduce_scatter x1, waiting for transfers between devices, body(): lax.psum_scatter(similarity_multiplier * jnp.einsum('pn,pd->nd', grad_ima...  123 us
    dot_general x1, matrix products, block_forward(): jnp.einsum('bsd,df->bsf', normed_two, w_expand, preferred_element_type=jn...  86.8 us
    all_gather x1, waiting for transfers between devices, body(): partner_all = lax.all_gather(partner, 'dp', axis=0, tiled=True)  58.4 us
    unnamed x1, blocking collectives  43.7 us
  transfers between devices with their start and end apart: 9, of which 8 were waited for; matrix products, arithmetic and copies ran while one was open for 5% of the time, Pallas kernels for 0%

commit v1 on v0

v1 whole, which is shorter than its diff:
```python
from functools import partial

import jax
import jax.numpy as jnp
import numpy as np
from jax import lax
from jax.experimental import pallas as pl
from jax.experimental.pallas import tpu as pltpu
from jax.sharding import PartitionSpec as P

F32 = jnp.float32
BF16 = jnp.bfloat16
HEAD_DIM = 64
LANES = 128
norm_eps = 1e-06
embed_eps = 1e-06
NEG = -1000000000.0
VMEM_LIMIT = 60 * 1024 * 1024
CDF_Q = (
    7.97884942e-01,
    3.63330840e-02,
    -3.25942309e-05,
    -5.53065609e-05,
    3.96482302e-06,
    -1.32270645e-07,
    1.75640958e-09,
)


def normal_cdf(x):
    sq = x * x
    q = CDF_Q[-1] * sq + CDF_Q[-2]
    for coef in CDF_Q[-3::-1]:
        q = q * sq + coef
    return 0.5 + 0.5 * jnp.tanh(x * q)


def dot(a, b):
    return jnp.dot(a, b, preferred_element_type=F32)


def dot_nt(a, b):
    return lax.dot_general(a, b, (((1,), (1,)), ((), ())), preferred_element_type=F32)


def dot_tn(a, b):
    return lax.dot_general(a, b, (((0,), (0,)), ((), ())), preferred_element_type=F32)


def norm_stats(x):
    mean = jnp.mean(x, axis=-1, keepdims=True)
    centered = x - mean
    rstd = lax.rsqrt(jnp.mean(centered * centered, axis=-1, keepdims=True) + norm_eps)
    return centered * rstd, rstd


def norm_back(dxhat, xhat, rstd):
    return rstd * (
        dxhat
        - jnp.mean(dxhat, axis=-1, keepdims=True)
        - xhat * jnp.mean(dxhat * xhat, axis=-1, keepdims=True)
    )


def row(ref, i):
    return ref[i : i + 1, :].astype(F32)


def head_masks():
    lane = lax.broadcasted_iota(jnp.int32, (1, LANES), 1)
    first = (lane < HEAD_DIM).astype(BF16)
    return first, (1 - first).astype(BF16)


def two_heads(x, masks):
    return jnp.concatenate([x * masks[0], x * masks[1]], axis=0)


def softmax_parts(scores, bias):
    keys = scores.shape[1] // 2
    parts = []
    for e in range(2):
        s = scores[:, e * keys : (e + 1) * keys] + bias
        parts.append(jnp.exp(s - jnp.max(s, axis=-1, keepdims=True)))
    return parts


def attend(q2, k2, v2, bias, masks):
    e0, e1 = softmax_parts(dot_nt(q2 * BF16(0.125), two_heads(k2, masks)), bias)
    weights = jnp.concatenate([e0.astype(BF16), e1.astype(BF16)], axis=1)
    ones = jnp.ones((k2.shape[0], LANES), BF16)
    right = jnp.concatenate([two_heads(v2, masks), two_heads(ones, masks)], axis=1)
    out = dot(weights, right)
    return (out[:, :LANES] / out[:, LANES:]).astype(BF16)


def split_dot(x, w):
    hi = x.astype(BF16)
    lo = (x - hi.astype(F32)).astype(BF16)
    n = x.shape[0]
    out = dot(jnp.concatenate([hi, lo], axis=0), w)
    return out[:n] + out[n:]


def text_forward_kernel(
    scal, h_any, gains, biases, hid, wq_any, wp_any, we_any, wr_any,
    a_out, qkv_out, o_out, m_out, c_out, gp_out, gs_out, emb_out, r_out,
    h_v, wq, wp, we, wr, av, cv, gsum, sems,
):
    n, width = m_out.shape
    caps = emb_out.shape[0]
    length = n // caps
    hidden = hid.shape[1]
    t = scal[0]
    copies = [
        pltpu.make_async_copy(h_any.at[pl.ds(pl.multiple_of(t * n, n), n)], h_v, sems.at[0]),
        pltpu.make_async_copy(wq_any, wq, sems.at[1]),
        pltpu.make_async_copy(wp_any, wp, sems.at[2]),
        pltpu.make_async_copy(we_any, we, sems.at[3]),
        pltpu.make_async_copy(wr_any, wr, sems.at[4]),
    ]
    for c in copies:
        c.start()
    copies[0].wait()
    masks = head_masks()
    blocks = width // a_out.shape[1]

    def put_transposed(out, value):
        turned = value.T.astype(BF16)
        rows = out.shape[1]
        for e in range(out.shape[0]):
            out[scal[4 + e]] = turned[e * rows : (e + 1) * rows, :]

    h = h_v[...].astype(F32)
    xhat, _ = norm_stats(h)
    a = xhat * row(gains, 0) + row(biases, 0)
    av[...] = a.astype(BF16)
    copies[1].wait()
    zero = jnp.zeros((1, width), F32)
    qkv_bias = (row(biases, 2), zero, row(biases, 3))
    for j in range(3 * width // 256):
        part, off = divmod(j * 256, width)
        bias = qkv_bias[part][:, off : off + 256]
        qkv_out[:, j * 256 : (j + 1) * 256] = (
            dot(av[...], wq[:, j * 256 : (j + 1) * 256]) + bias
        ).astype(BF16)
    put_transposed(a_out, a)
    same = (
        lax.broadcasted_iota(jnp.int32, (LANES, LANES), 0) // length
        == lax.broadcasted_iota(jnp.int32, (LANES, LANES), 1) // length
    )
    bias = jnp.where(same, 0.0, -1e30)

    def attention(g, carry):
        rows = pl.ds(pl.multiple_of(g * LANES, LANES), LANES)
        for p in range(width // LANES):
            lanes = slice(p * LANES, (p + 1) * LANES)
            q2 = qkv_out[rows, lanes]
            k2 = qkv_out[rows, width + p * LANES : width + (p + 1) * LANES]
            v2 = qkv_out[rows, 2 * width + p * LANES : 2 * width + (p + 1) * LANES]
            av[rows, lanes] = attend(q2, k2, v2, bias, masks)
        return carry

    lax.fori_loop(0, n // LANES, attention, 0)
    copies[2].wait()
    m = h + dot(av[...], wp[...]) + row(biases, 4)
    m_out[...] = m
    xhat, _ = norm_stats(m)
    c = xhat * row(gains, 1) + row(biases, 1)
    cv[...] = c.astype(BF16)
    copies[3].wait()

    def feed(j, carry):
        cols = pl.ds(pl.multiple_of(j * 256, 256), 256)
        f = dot(cv[...], we[:, cols]) + hid[:, cols].astype(F32)
        cdf = normal_cdf(f)
        density = jnp.exp(f * f * -0.5) * 0.3989422804014327
        gp_out[:, cols] = (cdf + f * density).astype(BF16)
        gelu = f * cdf
        gsum[:, cols] = jnp.sum(gelu.reshape(caps, length, 256), axis=1)
        return carry

    lax.fori_loop(0, hidden // 256, feed, 0)
    put_transposed(c_out, c)
    put_transposed(o_out, av[...].astype(F32))
    copies[4].wait()
    total = gsum[...]
    pooled = (
        jnp.mean(m_out[...].reshape(caps, length, width), axis=1)
        + split_dot(total * (1.0 / length), wr[...])
        + row(biases, 5)
    )
    r = lax.rsqrt(jnp.sum(pooled * pooled, axis=-1, keepdims=True) + embed_eps)
    emb_out[...] = pooled * r
    r_out[...] = jnp.broadcast_to(r, r_out.shape)
    gs_out[...] = (total * r).astype(BF16)


PAD = 56


def image_forward_kernel(
    scal, x_any, emb, r, gains, biases, hid, wq_any, wp_any, we_any, wr_any,
    out,
    x_v, hv, av, qkv, mv, msum, gsum, wq, wp, we, wr, sems,
):
    caps, length, width = x_v.shape
    n = caps * PAD
    hidden = hid.shape[1]
    t = scal[0]
    copies = [
        pltpu.make_async_copy(x_any.at[pl.ds(t * caps, caps)], x_v, sems.at[0]),
        pltpu.make_async_copy(wq_any, wq, sems.at[1]),
        pltpu.make_async_copy(wp_any, wp, sems.at[2]),
        pltpu.make_async_copy(we_any, we, sems.at[3]),
        pltpu.make_async_copy(wr_any, wr, sems.at[4]),
    ]
    for c in copies:
        c.start()
    masks = head_masks()
    qkv[n:, :] = jnp.zeros((qkv.shape[0] - n, 3 * width), BF16)
    copies[0].wait()

    def first_norm(j, carry):
        base = pl.multiple_of(j * 2 * PAD, 16)
        for e in range(2):
            x = x_v[j * 2 + e].astype(F32)
            x = jnp.concatenate([x, jnp.zeros((PAD - length, width), F32)], axis=0)
            hv[pl.ds(base + e * PAD, PAD), :] = x
        h = hv[pl.ds(base, 2 * PAD), :]
        xhat, _ = norm_stats(h)
        av[pl.ds(base, 2 * PAD), :] = (xhat * row(gains, 0) + row(biases, 0)).astype(BF16)
        return carry

    lax.fori_loop(0, caps // 2, first_norm, 0)
    copies[1].wait()
    zero = jnp.zeros((1, width), F32)
    qkv_bias = (row(biases, 2), zero, row(biases, 3))
    for j in range(3 * width // 256):
        part, off = divmod(j * 256, width)
        qkv[:n, j * 256 : (j + 1) * 256] = (
            dot(av[...], wq[:, j * 256 : (j + 1) * 256]) + qkv_bias[part][:, off : off + 256]
        ).astype(BF16)
    q_at = lax.broadcasted_iota(jnp.int32, (2 * PAD, LANES), 0)
    k_at = lax.broadcasted_iota(jnp.int32, (2 * PAD, LANES), 1)
    low = (q_at < PAD) & (k_at < length)
    high = (q_at >= PAD) & (k_at >= PAD) & (k_at < PAD + length)
    bias = jnp.where(low | high, 0.0, -1e30)

    def attention(j, carry):
        base = pl.multiple_of(j * 2 * PAD, 16)
        rows, keys = pl.ds(base, 2 * PAD), pl.ds(base, LANES)
        for p in range(width // LANES):
            lanes = slice(p * LANES, (p + 1) * LANES)
            q2 = qkv[rows, lanes]
            k2 = qkv[keys, width + p * LANES : width + (p + 1) * LANES]
            v2 = qkv[keys, 2 * width + p * LANES : 2 * width + (p + 1) * LANES]
            av[rows, lanes] = attend(q2, k2, v2, bias, masks)
        return carry

    lax.fori_loop(0, caps // 2, attention, 0)
    copies[2].wait()
    for j in range(width // 256):
        cols = slice(j * 256, (j + 1) * 256)
        mv[:, cols] = hv[:, cols] + dot(av[...], wp[:, cols]) + row(biases, 4)[:, cols]
    group = 8 * PAD
    tail = (lax.broadcasted_iota(jnp.int32, (1, 8, 1), 1) < length - (PAD - 8)).astype(F32)

    def token_sum(x, count):
        tiles = x.reshape(count, PAD // 8, 8, x.shape[1])
        acc = tiles[:, PAD // 8 - 1] * tail
        for i in range(PAD // 8 - 1):
            acc = acc + tiles[:, i]
        return jnp.sum(acc, axis=1)

    def second_norm(j, carry):
        rows = pl.ds(pl.multiple_of(j * group, 16), group)
        m = mv[rows, :]
        xhat, _ = norm_stats(m)
        av[rows, :] = (xhat * row(gains, 1) + row(biases, 1)).astype(BF16)
        msum[pl.ds(pl.multiple_of(j * 8, 8), 8), :] = token_sum(m, 8)
        return carry

    lax.fori_loop(0, caps // 8, second_norm, 0)
    copies[3].wait()

    def feed(j, carry):
        cols = pl.ds(pl.multiple_of(j * 256, 256), 256)
        f = dot(av[...], we[:, cols]) + hid[:, cols].astype(F32)
        gsum[:, cols] = token_sum(f * normal_cdf(f), caps)
        return carry

    lax.fori_loop(0, hidden // 256, feed, 0)
    copies[4].wait()
    scale = 1.0 / length
    pooled = msum[...] * scale + split_dot(gsum[...] * scale, wr[...]) + row(biases, 5)
    r_img = lax.rsqrt(jnp.sum(pooled * pooled, axis=-1, keepdims=True) + embed_eps)
    out[:, :width] = (pooled * r_img).astype(BF16)
    out[:, width : 2 * width] = emb[...].astype(BF16)
    rv = r[...]
    hi = rv.astype(BF16)
    mid = (rv - hi.astype(F32)).astype(BF16)
    lo = (rv - hi.astype(F32) - mid.astype(F32)).astype(BF16)
    lane = lax.broadcasted_iota(jnp.int32, rv.shape, 1)
    slot = lax.broadcasted_iota(jnp.int32, rv.shape, 0) + t * caps
    flag = jnp.where(slot < scal[2], 1.0, 0.0)
    extra = jnp.where(lane == 0, hi.astype(F32), 0.0)
    extra = jnp.where(lane == 1, mid.astype(F32), extra)
    extra = jnp.where(lane == 2, lo.astype(F32), extra)
    extra = jnp.where(lane == 3, flag, extra)
    out[:, 2 * width :] = extra.astype(BF16)


def loss_kernel(
    rows_block, scal, own_any, par_any, expo, emb, r, gall, gains, biases,
    gp_any, ct_any, m_any, we_any, wr_any,
    loss_out, temp_out, keep_out, send_out, dm_out, red_out, vec_out,
    own_v, par_v, texts, images, extra, col_flag, sims, grad_t, grad_i, dt_v, dt_own,
    gp, ct, mv, we, wr, dc, exp_s, sems,
):
    chips, caps, _ = own_any.shape
    staged = own_v.shape[0] == chips
    total, width = texts.shape
    hidden = gp.shape[1]
    n = mv.shape[0]
    length = n // caps
    t, d = scal[0], scal[1]
    loads = [
        pltpu.make_async_copy(src, dst, sems.at[i])
        for i, (src, dst) in enumerate(
            ((own_any, own_v), (par_any, par_v), (wr_any, wr), (we_any, we), (gp_any, gp),
             (ct_any, ct), (m_any, mv))
        )
        if staged or i > 1
    ]
    for c in loads:
        c.start()
    if staged:
        loads[0].wait()
        loads[1].wait()
        loads = loads[2:]
    first = (jnp.zeros((1, 1), jnp.int32) + t) == 0

    def place(e, carry):
        slot = scal[4 + 16 + e]
        if not staged:
            for i, (src, dst) in enumerate(((own_any, own_v), (par_any, par_v))):
                one = pltpu.make_async_copy(src.at[pl.ds(slot, 1)], dst, sems.at[i])
                one.start()
                one.wait()
            slot = 0
        x0 = own_v[slot].astype(F32)
        x1 = par_v[slot].astype(F32)
        both = jnp.concatenate([jnp.where(first, x0, x1), jnp.where(first, x1, x0)], axis=0)
        rows = pl.ds(pl.multiple_of(e * 2 * caps, 16), 2 * caps)
        images[rows, :] = both[:, :width].astype(BF16)
        texts[rows, :] = both[:, width : 2 * width].astype(BF16)
        extra[rows, :] = both[:, 2 * width :]
        return carry

    lax.fori_loop(0, chips, place, 0)
    pick = (lax.broadcasted_iota(jnp.int32, (8, LANES), 1) == 3).astype(F32)
    step = min(256, total)

    def flags(j, carry):
        cols = pl.ds(pl.multiple_of(j * step, step), step)
        col_flag[:, cols] = dot_nt(pick, extra[cols, :])
        return carry

    lax.fori_loop(0, total // step, flags, 0)
    scale = jnp.exp(jnp.full((1, 1), expo[0], F32))
    chunk = 48
    blocks = total // rows_block

    def similarities(b):
        base = pl.multiple_of(b * rows_block, 16)

        def cols_step(j, carry):
            cols = pl.ds(pl.multiple_of(j * step, step), step)
            sims[:, cols] = scale * dot_nt(texts[pl.ds(base, rows_block), :], images[cols, :])
            return carry

        lax.fori_loop(0, total // step, cols_step, 0)

    def chunk_at(b, i):
        local = pl.ds(pl.multiple_of(i * chunk, 16), chunk)
        whole = pl.ds(pl.multiple_of(b * rows_block + i * chunk, 16), chunk)
        return local, whole

    per_block = rows_block // chunk
    col_max = jnp.full((1, total), NEG, F32)
    col_sum = jnp.zeros((1, total), F32)

    def column_block(b, carry):
        cm, cs = carry
        similarities(b)

        def peak(i, best):
            local, whole = chunk_at(b, i)
            live = extra[whole, 3:4] > 0.0
            return jnp.maximum(
                best, jnp.max(jnp.where(live, sims[local, :], NEG), axis=0, keepdims=True)
            )

        new = lax.fori_loop(0, per_block, peak, cm)

        def adding(i, acc):
            local, whole = chunk_at(b, i)
            live = extra[whole, 3:4] > 0.0
            return acc + jnp.sum(
                jnp.exp(jnp.where(live, sims[local, :], NEG) - new), axis=0, keepdims=True
            )

        return new, lax.fori_loop(0, per_block, adding, cs * jnp.exp(cm - new))

    if blocks == 1:
        col_max, col_sum = column_block(0, (col_max, col_sum))
    else:
        col_max, col_sum = lax.fori_loop(0, blocks, column_block, (col_max, col_sum))
    col_live = col_flag[0:1, :] > 0.0
    col_half = 0.5 * col_flag[0:1, :]
    col_lse = col_max + jnp.log(col_sum)
    inv_col = 1.0 / col_sum

    def row_block(b, carry):
        if blocks > 1:
            similarities(b)

        def rows_step(i, acc):
            loss, temp, rb = acc
            local, whole = chunk_at(b, i)
            s = sims[local, :]
            flag = extra[whole, 3:4]
            at = lax.broadcasted_iota(jnp.int32, (chunk, total), 0) + (b * rows_block + i * chunk)
            eye = (at == lax.broadcasted_iota(jnp.int32, (chunk, total), 1)).astype(F32)
            masked = jnp.where(col_live, s, NEG)
            top = jnp.max(masked, axis=1, keepdims=True)
            expd = jnp.exp(masked - top)
            rsum = jnp.sum(expd, axis=1, keepdims=True)
            gt = (0.5 * flag * (expd * (1.0 / rsum) - eye)).astype(BF16)
            expc = jnp.exp(jnp.where(flag > 0.0, s, NEG) - col_max) * inv_col
            gi = (col_half * (expc - eye)).astype(BF16)
            grad_t[local, :] = gt
            grad_i[local, :] = gi
            both = gt.astype(F32) + gi.astype(F32)
            temp = temp + jnp.sum(both * s, axis=0, keepdims=True)
            diag = jnp.sum(eye * s, axis=1, keepdims=True)
            loss = loss + flag * (0.5 * (top + jnp.log(rsum)) - diag)
            return loss, temp, rb

        loss, temp, rb = lax.fori_loop(0, per_block, rows_step, carry)
        dt_v[...] = scale * (dot(grad_t[...], images[...]) + dot(grad_i[...], images[...]))

        def project(i, rb):
            local, whole = chunk_at(b, i)
            dt = dt_v[local, :]
            tx = texts[whole, :].astype(F32)
            part = (dt - tx * jnp.sum(tx * dt, axis=1, keepdims=True)) * (1.0 / length)
            part = part.astype(BF16)
            texts[whole, :] = part
            inv = extra[whole, 0:1] + extra[whole, 1:2] + extra[whole, 2:3]
            return rb + jnp.sum(part.astype(F32) * inv, axis=0, keepdims=True)

        rb = lax.fori_loop(0, per_block, project, rb)
        mine = d * (2 * caps) + t * caps - b * rows_block

        @pl.when((mine >= 0) & (mine < rows_block))
        def _():
            dt_own[...] = dt_v[pl.ds(pl.multiple_of(mine, 8), caps), :]

        return loss, temp, rb

    start = (jnp.zeros((chunk, 1), F32), jnp.zeros((1, total), F32), jnp.zeros((1, width), F32))
    if blocks == 1:
        loss, temp, rb = row_block(0, start)
    else:
        loss, temp, rb = lax.fori_loop(0, blocks, row_block, start)
    objective = jnp.sum(loss, axis=0, keepdims=True) + jnp.sum(
        col_half * col_lse, axis=1, keepdims=True
    )
    valid_count = jnp.sum(col_flag[0:1, :], axis=1, keepdims=True)
    loss_out[...] = jnp.broadcast_to(objective / valid_count, loss_out.shape)
    temp_out[...] = jnp.broadcast_to(jnp.sum(temp, axis=1, keepdims=True), temp_out.shape)

    tx = emb[...]
    dt = dt_own[...]
    dy = r[:, 0:1] * (dt - tx * jnp.sum(tx * dt, axis=1, keepdims=True)) * (1.0 / length)
    dyb = dy.astype(BF16)
    for c in loads[:4]:
        c.wait()
    dc[...] = jnp.zeros_like(dc)

    def feed(j, carry):
        cols = pl.ds(pl.multiple_of(j * 256, 256), 256)
        dg = dot_nt(dyb, wr[cols, :])
        df = gp[:, cols].astype(F32).reshape(caps, length, 256) * dg[:, None, :]
        df = df.reshape(n, 256).astype(BF16)
        per_row = width // 256
        vec_out[pl.ds(4 + j // per_row, 1), pl.ds(pl.multiple_of((j % per_row) * 256, 256), 256)] = (
            jnp.sum(df.astype(F32), axis=0, keepdims=True)
        )
        dc[...] += dot_nt(df, we[:, cols])
        half = hidden // 512
        out_cols = pl.ds(pl.multiple_of((j % half) * 256, 256), 256)
        exp_s[j // half, :, out_cols] = dot(ct[...].reshape(width, n), df).astype(BF16)
        return carry

    lax.fori_loop(0, hidden // 256, feed, 0)
    stores = [
        pltpu.make_async_copy(exp_s.at[t], keep_out, sems.at[0]),
        pltpu.make_async_copy(exp_s.at[1 - t], send_out, sems.at[1]),
    ]
    for c in stores:
        c.start()
    red_out[...] = dot_tn(gall[...], texts[...])
    loads[4].wait()
    xhat, rstd = norm_stats(mv[...])
    dcv = dc[...]
    vec_out[0:1, :] = jnp.sum(dcv * xhat, axis=0, keepdims=True)
    vec_out[1:2, :] = jnp.sum(dcv, axis=0, keepdims=True)
    back = norm_back(dcv * row(gains, 1), xhat, rstd)
    dm = (back.reshape(caps, length, width) + dy[:, None, :]).reshape(n, width)
    dm_out[...] = dm
    vec_out[2:3, :] = jnp.sum(dm.astype(BF16).astype(F32), axis=0, keepdims=True)
    vec_out[3:4, :] = rb * float(length)
    for c in stores:
        c.wait()


def attention_back_kernel(
    scal, dm, h_any, gains, biases, qkv, at, ot, wp_any, wq_any,
    keep_out, send_out, tok_keep, tok_send, vec_out,
    h_v, wp, wq, dmb, dov, dqkv, grads, sems,
):
    n, width = dm.shape
    caps, half_len, _ = tok_keep.shape
    length = 2 * half_len
    t = scal[0]
    loads = [
        pltpu.make_async_copy(wp_any, wp, sems.at[0]),
        pltpu.make_async_copy(wq_any, wq, sems.at[1]),
        pltpu.make_async_copy(h_any.at[pl.ds(pl.multiple_of(t * n, n), n)], h_v, sems.at[2]),
    ]
    for c in loads:
        c.start()
    masks = head_masks()
    same = (
        lax.broadcasted_iota(jnp.int32, (LANES, LANES), 0) // length
        == lax.broadcasted_iota(jnp.int32, (LANES, LANES), 1) // length
    )
    bias = jnp.where(same, 0.0, -1e30)
    dmb[...] = dm[...].astype(BF16)
    loads[0].wait()
    dov[...] = dot_nt(dmb[...], wp[...]).astype(BF16)

    def attention(g, carry):
        rows = pl.ds(pl.multiple_of(g * LANES, LANES), LANES)
        for p in range(width // LANES):
            lanes = slice(p * LANES, (p + 1) * LANES)
            k_lanes = slice(width + p * LANES, width + (p + 1) * LANES)
            v_lanes = slice(2 * width + p * LANES, 2 * width + (p + 1) * LANES)
            q2 = qkv[rows, lanes] * BF16(0.125)
            km = two_heads(qkv[rows, k_lanes], masks)
            vm = two_heads(qkv[rows, v_lanes], masks)
            do2 = dov[rows, lanes]
            parts = softmax_parts(dot_nt(q2, km), bias)
            dp = dot_nt(do2, vm)
            pb, ds = [], []
            for e in range(2):
                prob = parts[e] * (1.0 / jnp.sum(parts[e], axis=-1, keepdims=True))
                dpe = dp[:, e * LANES : (e + 1) * LANES]
                inner = jnp.sum(prob * dpe, axis=-1, keepdims=True)
                pb.append(prob.astype(BF16))
                ds.append((prob * (dpe - inner)).astype(BF16))
            dqkv[rows, lanes] = (dot(jnp.concatenate(ds, axis=1), km) * 0.125).astype(BF16)
            dqkv[rows, k_lanes] = dot_tn(jnp.concatenate(ds, axis=0), two_heads(q2, masks)).astype(
                BF16
            )
            dqkv[rows, v_lanes] = dot_tn(
                jnp.concatenate(pb, axis=0), two_heads(do2, masks)
            ).astype(BF16)
        return carry

    lax.fori_loop(0, n // LANES, attention, 0)
    half = width // 2
    otv = ot[...].reshape(width, n)
    atv = at[...].reshape(width, n)
    for hh in range(2):
        grads[hh, :, :half] = dot(otv, dmb[:, hh * half : (hh + 1) * half]).astype(BF16)
        for j in range(3):
            src = hh * 3 * half + j * half
            grads[hh, :, (j + 1) * half : (j + 2) * half] = dot(
                atv, dqkv[:, src : src + half]
            ).astype(BF16)
    stores = [
        pltpu.make_async_copy(grads.at[t], keep_out, sems.at[3]),
        pltpu.make_async_copy(grads.at[1 - t], send_out, sems.at[4]),
    ]
    for c in stores:
        c.start()
    loads[1].wait()
    loads[2].wait()
    da = dot_nt(dqkv[...], wq[...])
    xhat, rstd = norm_stats(h_v[...].astype(F32))
    vec_out[0:1, :] = jnp.sum(da * xhat, axis=0, keepdims=True)
    vec_out[1:2, :] = jnp.sum(da, axis=0, keepdims=True)
    vec_out[2:3, :] = jnp.sum(dqkv[:, :width].astype(F32), axis=0, keepdims=True)
    vec_out[3:4, :] = jnp.sum(dqkv[:, 2 * width :].astype(F32), axis=0, keepdims=True)
    vec_out[4:8, :] = jnp.zeros((4, width), F32)
    grad = dm[...] + norm_back(da * row(gains, 0), xhat, rstd)
    halves = grad.reshape(caps, 2, half_len, width)
    first = (jnp.zeros((1, 1, 1), jnp.int32) + t) == 0
    tok_keep[...] = jnp.where(first, halves[:, 0], halves[:, 1])
    tok_send[...] = jnp.where(first, halves[:, 1], halves[:, 0]).astype(BF16)
    for c in stores:
        c.wait()


def xor_permute(x, axis, bit):
    return lax.ppermute(x, axis, [(i, i ^ bit) for i in range(lax.axis_size(axis))])


def bit_groups(count):
    bits = [1 << i for i in range(count.bit_length() - 1)]
    groups = [tuple(bits[i : i + 2]) for i in range(0, len(bits), 2)]
    return groups[::-1]


def reaches(group):
    out = [0]
    for bit in group:
        out = out + [r ^ bit for r in out]
    return out


def slot_reaches(count):
    order = [0]
    for group in bit_groups(count):
        order = [r ^ o for r in reaches(group) for o in order]
    return order


def gather_slots(x, count):
    y = x[None]
    for group in bit_groups(count):
        y = jnp.concatenate(
            [y if r == 0 else xor_permute(y, "dp", r) for r in reaches(group)], axis=0
        )
    return y


def scatter_sum(s, count, to_wire, from_wire):
    for group in reversed(bit_groups(count)):
        hops = reaches(group)
        rows = s.shape[0] // len(hops)
        parts = [s[i * rows : (i + 1) * rows] for i in range(len(hops))]
        moved = [xor_permute(to_wire(parts[i]), "dp", r) for i, r in enumerate(hops) if r]
        s = parts[0]
        for piece in moved:
            s = s + from_wire(piece)
    return s


def flip_by(x, index, count):
    for i in range(count.bit_length() - 1):
        bit = 1 << i
        shape = x.shape
        pairs = x.reshape((count // (2 * bit), 2, bit) + shape[1:])
        x = jnp.where((index & bit) != 0, pairs[:, ::-1], pairs).reshape(shape)
    return x


SMEM = pl.BlockSpec(memory_space=pltpu.SMEM)
VMEM = pl.BlockSpec(memory_space=pltpu.VMEM)
ANY = pl.BlockSpec(memory_space=pl.ANY)


def call(kernel, name, in_specs, outs, out_specs, scratch, args, flops, moved):
    return pl.pallas_call(
        kernel,
        name=name,
        in_specs=in_specs,
        out_shape=[jax.ShapeDtypeStruct(s, d) for s, d in outs],
        out_specs=out_specs,
        scratch_shapes=scratch,
        compiler_params=pltpu.CompilerParams(vmem_limit_bytes=VMEM_LIMIT),
        cost_estimate=pl.CostEstimate(flops=flops, bytes_accessed=moved, transcendentals=0),
    )(*args)


def body(
    pictures, captions, tallies, exponent,
    p_gains, p_biases, p_hid, p_wq, p_wp, p_we, p_wr,
    c_gains, c_biases, c_hid, c_wq, c_wp, c_we, c_wr,
):
    t = lax.axis_index("tower")
    d = lax.axis_index("dp")
    chips = lax.axis_size("dp")
    pairs, length, width = captions.shape
    img_len = pictures.shape[1]
    hidden = c_hid.shape[0]
    caps = pairs // 2
    n = caps * length
    total = pairs * chips
    row_blocks = 16
    order = np.array(slot_reaches(chips))
    slot_of = np.zeros(chips, np.int32)
    slot_of[order] = np.arange(chips)
    table = np.stack([slot_of[np.arange(chips) ^ i] for i in range(chips)]).astype(np.int32)
    slots = lax.dynamic_slice_in_dim(jnp.asarray(table), d, 1, 0)[0]
    relative = chips == row_blocks
    row_slots = slots if relative else jnp.arange(row_blocks, dtype=jnp.int32)
    head = jnp.stack([t, d, tallies[0], t]).astype(jnp.int32)
    scal = jnp.concatenate([head, row_slots, slots])

    texts_in = captions.reshape(pairs * length, width)
    c_hid2, p_hid2 = c_hid.reshape(1, hidden), p_hid.reshape(1, hidden)
    blk = (row_blocks, width // row_blocks, n)
    vm = pltpu.VMEM
    a_t, qkv, o_t, m, c_t, gp, gs, emb, r = call(
        text_forward_kernel, "text_forward",
        [SMEM, ANY, VMEM, VMEM, VMEM, ANY, ANY, ANY, ANY],
        [(blk, BF16), ((n, 3 * width), BF16), (blk, BF16), ((n, width), F32), (blk, BF16),
         ((n, hidden), BF16), ((caps, hidden), BF16), ((caps, width), F32), ((caps, LANES), F32)],
        [VMEM] * 9,
        [vm((n, width), BF16), vm((width, 3 * width), BF16), vm((width, width), BF16),
         vm((width, hidden), BF16), vm((hidden, width), BF16), vm((n, width), BF16),
         vm((n, width), BF16), vm((caps, hidden), F32), pltpu.SemaphoreType.DMA((5,))],
        (scal, texts_in, c_gains, c_biases, c_hid2, c_wq, c_wp, c_we, c_wr),
        int(2 * n * width * (4 * width + hidden)), 20_000_000,
    )

    share = hidden // (2 * chips)
    pieces = jnp.transpose(gs.reshape(caps, 2, chips, share), (2, 0, 1, 3))
    pieces = lax.all_to_all(pieces, "dp", 0, 0, tiled=True)
    g_mine = jnp.where(t == 0, pieces[:, :, 0], pieces[:, :, 1])
    g_other = jnp.where(t == 0, pieces[:, :, 1], pieces[:, :, 0])
    g_back = xor_permute(g_other, "tower", 1)
    g_all = jnp.concatenate(
        [jnp.where(t == 0, g_mine, g_back), jnp.where(t == 0, g_back, g_mine)], axis=1
    ).reshape(total, share)

    rows = caps * PAD
    (payload,) = call(
        image_forward_kernel, "image_forward",
        [SMEM, ANY, VMEM, VMEM, VMEM, VMEM, VMEM, ANY, ANY, ANY, ANY],
        [((caps, 2 * width + LANES), BF16)],
        [VMEM],
        [vm((caps, img_len, width), BF16), vm((rows, width), F32), vm((rows, width), BF16),
         vm((rows + 16, 3 * width), BF16), vm((rows, width), F32), vm((caps, width), F32),
         vm((caps, hidden), F32), vm((width, 3 * width), BF16), vm((width, width), BF16),
         vm((width, hidden), BF16), vm((hidden, width), BF16), pltpu.SemaphoreType.DMA((5,))],
        (scal, pictures, emb, r, p_gains, p_biases, p_hid2, p_wq, p_wp, p_we, p_wr),
        int(2 * rows * width * (4 * width + hidden)), 20_000_000,
    )
    own_all = gather_slots(payload, chips)
    par_all = xor_permute(own_all, "tower", 1)

    block = total if total <= 768 else 96
    staging = (chips if total <= 768 else 1,) + payload.shape
    loss, temp, e_keep, e_send, dm, reduce_grad, vec_ff = call(
        partial(loss_kernel, block), "loss_and_feed_back",
        [SMEM, ANY, ANY, SMEM, VMEM, VMEM, VMEM, VMEM, VMEM, ANY, ANY, ANY, ANY, ANY],
        [((8, LANES), F32), ((8, LANES), F32), ((width, hidden // 2), BF16),
         ((width, hidden // 2), BF16), ((n, width), F32), ((share, width), F32), ((8, width), F32)],
        [VMEM, VMEM, ANY, ANY, VMEM, VMEM, VMEM],
        [vm(staging, BF16), vm(staging, BF16), vm((total, width), BF16),
         vm((total, width), BF16), vm((total, LANES), F32), vm((8, total), F32),
         vm((block, total), F32), vm((block, total), BF16), vm((block, total), BF16),
         vm((block, width), F32), vm((caps, width), F32),
         vm((n, hidden), BF16), vm(blk, BF16), vm((n, width), F32), vm((width, hidden), BF16),
         vm((hidden, width), BF16), vm((n, width), F32), vm((2, width, hidden // 2), BF16),
         pltpu.SemaphoreType.DMA((7,))],
        (scal, own_all, par_all, exponent, emb, r, g_all, c_gains, c_biases, gp, c_t, m, c_we, c_wr),
        int(4 * n * width * hidden), 20_000_000,
    )

    q_keep, q_send, tok_keep, tok_send, vec_at = call(
        attention_back_kernel, "attention_back",
        [SMEM, VMEM, ANY, VMEM, VMEM, VMEM, VMEM, VMEM, ANY, ANY],
        [((width, 2 * width), BF16), ((width, 2 * width), BF16),
         ((caps, length // 2, width), F32), ((caps, length // 2, width), BF16), ((8, width), F32)],
        [ANY, ANY, VMEM, VMEM, VMEM],
        [vm((n, width), BF16), vm((width, width), BF16), vm((width, 3 * width), BF16),
         vm((n, width), BF16), vm((n, width), BF16), vm((n, 3 * width), BF16),
         vm((2, width, 2 * width), BF16), pltpu.SemaphoreType.DMA((5,))],
        (scal, dm, texts_in, c_gains, c_biases, qkv, a_t, o_t, c_wp, c_wq),
        int(2 * n * width * 8 * width), 20_000_000,
    )

    def by_slot(x):
        if relative:
            return x
        x = flip_by(x.reshape((chips, width // chips) + x.shape[1:]), d, chips)
        return x[order].reshape((width,) + x.shape[2:])

    e_back = xor_permute(e_send, "tower", 1)
    e_sum = by_slot(e_keep.astype(F32) + e_back.astype(F32))
    expand_grad = scatter_sum(e_sum, chips, lambda x: x.astype(BF16), lambda x: x.astype(F32))

    tok_back = xor_permute(tok_send, "tower", 1).astype(F32)
    grad_tokens = jnp.concatenate(
        [jnp.where(t == 0, tok_keep, tok_back), jnp.where(t == 0, tok_back, tok_keep)], axis=0
    )

    zero = jnp.zeros((1, width), F32)
    for_zero = jnp.concatenate([vec_at[0:2], vec_ff[1:2], vec_at[2:3], vec_ff[4:6]])
    for_one = jnp.concatenate([vec_ff[0:1], vec_at[3:4], vec_ff[2:3], zero, vec_ff[6:8]])
    v_keep = jnp.where(t == 0, for_zero, for_one)
    v_send = jnp.where(t == 0, for_one, for_zero)
    v_sum = v_keep + xor_permute(v_send, "tower", 1)
    cols = width // chips
    lead = jnp.transpose(v_sum[:4].reshape(4, chips, cols), (1, 2, 0))
    tail = jnp.transpose(v_sum[4:].reshape(chips, 2, cols), (0, 2, 1))
    small = jnp.concatenate([lead, tail], axis=2)
    small = flip_by(small, d, chips)[order].reshape(width, 6)
    small = jnp.pad(small, ((0, 0), (0, LANES // 2 - 6)))

    q_back = xor_permute(q_send, "tower", 1)
    q_sum = by_slot(q_keep.astype(F32) + q_back.astype(F32))
    wide = q_sum.shape[1]
    q_full = jnp.concatenate([q_sum, small], axis=1)

    def q_to_wire(x):
        hi = x.astype(BF16)
        s = x[:, wide:]
        lo = (s - s.astype(BF16).astype(F32)).astype(BF16)
        return jnp.concatenate([hi, lo], axis=1)

    def q_from_wire(x):
        y = x.astype(F32)
        return jnp.concatenate([y[:, :wide], y[:, wide : wide + 64] + y[:, wide + 64 :]], axis=1)

    q_grad = scatter_sum(q_full, chips, q_to_wire, q_from_wire)
    half = width // 2
    project_grad, qkv_grad = q_grad[:, :half], q_grad[:, half:wide]
    small = q_grad[:, wide : wide + 6]
    gains_grad = small[:, 0].reshape(1, cols)
    rbias = lax.dynamic_slice_in_dim(vec_ff[3], d * cols, cols, 0)
    last = jnp.where(t == 0, small[:, 3], rbias)
    biases_grad = jnp.stack([small[:, 1], small[:, 2], last])
    hid_grad = small[:, 4:6].T.reshape(2 * cols)
    return (
        loss[0, :1], temp[0, :1], grad_tokens, gains_grad, biases_grad, hid_grad,
        qkv_grad, project_grad, expand_grad, reduce_grad,
    )


def solution(mesh):
    in_specs = (P("dp", None, None), P("dp", None, None), P("dp")) + (P(),) * 15
    out_specs = (
        P(), P(), P("dp", "tower", None), P("tower", "dp"), P("tower", "dp"),
        P(("tower", "dp")), P("dp", "tower"), P("dp", "tower"), P("dp", "tower"),
        P(("tower", "dp"), None),
    )
    return jax.shard_map(body, mesh=mesh, in_specs=in_specs, out_specs=out_specs, check_vma=False)
```

time: 1300 us -> 258 us (0.20)
  waiting for transfers between devices: 628 us -> 80.2 us
  blocking collectives: 273 us -> 0 us
  matrix products: 164 us -> 0 us
  local copies, waits for them, and re-layouts: 141 us -> 22.2 us
  Pallas kernels: 0 us -> 110 us
  starting transfers between devices: 0.4 us -> 31.1 us
  other arithmetic: 41.3 us -> 11.3 us
  loops' own time: 19.7 us -> 0 us
  between operations: 21.4 us -> 2.49 us
    reduce_scatter x5 -> x0, waiting for transfers between devices: 559 us -> none  [the longest x1 142 us: body(): lax.psum_scatter(a_reduce, ('tower', 'dp'), scatter_dimension=0, tiled=True)]
    psum x1 -> x0, blocking collectives: 229 us -> none  [body(): lax.psum((loss_portion, warmth_portion), ('tower', 'dp'))]
    dot_general x10 -> x0, matrix products: 164 us -> none  [the longest x1 86.8 us: block_forward(): jnp.einsum('bsd,df->bsf', normed_two, w_expand, preferred_element_type=jn...]
    pallas_call x0 -> x4, Pallas kernels: none -> 110 us  [call(): pl.pallas_call(kernel, name=name, in_specs=in_specs, out_shape=[jax.Shape...]
    reshape x14 -> x7, local copies, waits for them, and re-layouts: 93.9 us -> 3.67 us  [the longest x2 1.91 us: body(): c_hid2, p_hid2 = (c_hid.reshape(1, hidden), p_hid.reshape(1, hidden))]
    ppermute x1 -> x24, waiting for transfers between devices: 1.46 us -> 71.3 us  [xor_permute(): lax.ppermute(x, axis, [(i, i ^ bit) for i in range(lax.axis_size(axis))])]
    all_gather x2 -> x0, waiting for transfers between devices: 67.3 us -> none  [the longest x1 58.4 us: body(): partner_all = lax.all_gather(partner, 'dp', axis=0, tiled=True)]
    unnamed x1 -> x0, blocking collectives: 43.7 us -> none
  transfers between devices with their start and end apart: 9 -> 25, of which waited for: 8 -> 12; matrix products, arithmetic and copies ran while one was open for 5% -> 7% of each run, Pallas kernels for 0% -> 8%
where the time goes in v1:
time: 258 us; the launch traced here: 257 us
  Pallas kernels  110 us (43%)
  waiting for transfers between devices  80.2 us (31%)
  starting transfers between devices  31.1 us (12%)
  local copies, waits for them, and re-layouts  22.2 us (9%)
  other arithmetic  11.3 us (4%)
    pallas_call x4, Pallas kernels, call(): pl.pallas_call(kernel, name=name, in_specs=in_specs, out_shape=[jax.Shape...  110 us
    ppermute x24, waiting for transfers between devices, xor_permute(): lax.ppermute(x, axis, [(i, i ^ bit) for i in range(lax.axis_size(axis))])  71.3 us
    ppermute x24, starting transfers between devices, xor_permute(): lax.ppermute(x, axis, [(i, i ^ bit) for i in range(lax.axis_size(axis))])  25.6 us
    all_to_all x1, waiting for transfers between devices, body(): pieces = lax.all_to_all(pieces, 'dp', 0, 0, tiled=True)  8.92 us
    unnamed x25, local copies, waits for them, and re-layouts  8.42 us
    all_to_all x1, starting transfers between devices, body(): pieces = lax.all_to_all(pieces, 'dp', 0, 0, tiled=True)  5.48 us
  transfers between devices with their start and end apart: 25, of which 12 were waited for; matrix products, arithmetic and copies ran while one was open for 7% of the time, Pallas kernels for 8%

profile of v1, /device:TPU:0, one launch (start us, length us, event | category | flops | bytes accessed | tf_op | source)
XLA Modules:
  0.0 257.3 jit_solution(13687164521661484273)
XLA Ops:
  1.3 1.3 reshape.60.hid
  2.6 5.3 %copy.41.x_any = bf16[48,50,768]{2,1,0:T(8,128)(2,1)} copy(bf16[48,50,768]{2,0,1:T(8,128)(2,1)} %param.21) | data formatting | bytes 7372800 | tf_op args[0]
  9.8 18.3 %text_forward.1 = (bf16[16,48,384]{2,1,0:T(8,128)(2,1)}, bf16[384,2304]{1,0:T(8,128)(2,1)}, bf16[16,48,384]{2,1,0:T(8,128)(2,1)}, f32[384,768]{1,0:T(8,128)}, bf...) custom-call(s32[36]{0:T(128)} %concatenate.64.scal, ...), custom_call_target="tpu_custom_call" | custom-call | flops 3623878656 | bytes 20000000 | tf_op jit(solution)/shard_map/text_forward/pallas_call | solution.py:679
  28.1 39.2 %image_forward.1 = bf16[24,1664]{1,0:T(8,128)(2,1)} custom-call(s32[36]{0:T(128)} %concatenate.64.scal, bf16[48,50,768]{2,1,0:T(8,128)(2,1)} %copy.41.x_any, f32[24,768]{1,0:T(8,128)} %get-tuple-element.31.emb, f32[24,128]{1,0:T(8,128)} %get-tuple-element.32.r, bf16[2,768]{1,0:T(2,128)(2,1)} %gains.5, bf16[6,768]{1,0:T(8,128)(2,1)} %biases.5, ...), custom_call_target="tpu_custom_call" | custom-call | flops 12683575296 | bytes 20000000 | tf_op jit(solution)/shard_map/image_forward/pallas_call | solution.py:679
  67.4 3.1 %collective-permute-start = (bf16[1,24,1664]{2,1,0:T(8,128)(2,1)}, bf16[1,24,1664]{2,1,0:T(8,128)(2,1)S(1)}, u32[]{:S(2)}, u32[]{:S(2)}) collective-permute-start(bf16[1,24,1664]{2,1,0:T(8,128)(2,1)} %bitcast.67), channel_id=1, source_target_pairs={{0,4},{1,5},{2,6},{3,7},{4,0},{5,1},{6,2},{7,3},{8,12},{9,13},{10,... | collective-permute-start | bytes 239624 | tf_op jit(solution)/shard_map/ppermute | solution.py:620
  70.5 2.6 %collective-permute-start.1 = (bf16[1,24,1664]{2,1,0:T(8,128)(2,1)}, bf16[1,24,1664]{2,1,0:T(8,128)(2,1)S(1)}, u32[]{:S(2)}, u32[]{:S(2)}) collective-permute-start(bf16[1,24,1664]{2,1,0:T(8,128)(2,1)} %bitcast.68), channel_id=1, source_target_pairs={{0,8},{1,9},{2,10},{3,11},{4,12},{5,13},{6,14},{7,15},{8,0},{9,1},... | collective-permute-start | bytes 239624 | tf_op jit(solution)/shard_map/ppermute | solution.py:620
  74.0 5.7 %collective-permute-done.1 = bf16[1,24,1664]{2,1,0:T(8,128)(2,1)S(1)} collective-permute-done((bf16[1,24,1664]{2,1,0:T(8,128)(2,1)}, bf16[1,24,1664]{2,1,0:T(8,128)(2,1)S(1)}, u32[]{:S(2)}, u32[]{:S(2)}) %collective-permute-start.1) | collective-permute-done | bytes 79904 | tf_op jit(solution)/shard_map/ppermute | solution.py:620
  80.7 1.6 collective-permute-start.3
  82.2 1.5 collective-permute-start.4
  84.3 6.9 %collective-permute-done.3 = bf16[4,24,1664]{2,1,0:T(8,128)(2,1)S(1)} collective-permute-done((bf16[4,24,1664]{2,1,0:T(8,128)(2,1)S(1)}, bf16[4,24,1664]{2,1,0:T(8,128)(2,1)S(1)}, u32[]{:S(2)}, u32[]{:S(2)}) %collective-permute-start.3) | collective-permute-done | bytes 319520 | tf_op jit(solution)/shard_map/ppermute | solution.py:620
  91.3 4.9 %collective-permute-done.4 = bf16[4,24,1664]{2,1,0:T(8,128)(2,1)S(1)} collective-permute-done((bf16[4,24,1664]{2,1,0:T(8,128)(2,1)S(1)}, bf16[4,24,1664]{2,1,0:T(8,128)(2,1)S(1)}, u32[]{:S(2)}, u32[]{:S(2)}) %collective-permute-start.4) | collective-permute-done | bytes 319520 | tf_op jit(solution)/shard_map/ppermute | solution.py:620
  97.4 5.5 %all-to-all-start = ((bf16[16,24,2,96]{3,1,2,0:T(8,128)(2,1)}), bf16[16,24,2,96]{3,1,2,0:T(8,128)(2,1)S(1)}, u32[]{:S(2)}, u32[]{:S(2)}) async-start(bf16[16,24,2,96]{3,1,2,0:T(8,128)(2,1)} %bitcast.55), calls=%async_computation | async-start | bytes 393216 | tf_op jit(solution)/shard_map/all_to_all | solution.py:735
  102.9 8.9 %all-to-all-done = bf16[16,24,2,96]{3,1,2,0:T(8,128)(2,1)S(1)} async-done(((bf16[16,24,2,96]{3,1,2,0:T(8,128)(2,1)}), bf16[16,24,2,96]{3,1,2,0:T(8,128)(2,1)S(1)}, u32[]{:S(2)}, u32[]{:S(2)}) %all-to-all-start) | async-done | bytes 147488 | tf_op jit(solution)/shard_map/all_to_all | solution.py:735
  115.0 32.1 %loss_and_feed_back.1 = (f32[8,128]{1,0:T(8,128)}, f32[8,128]{1,0:T(8,128)}, bf16[768,1536]{1,0:T(8,128)(2,1)}, bf16[768,1536]{1,0:T(8,128)(2,1)}, f32[384,768]{...) custom-call(s32[36]{0:T(128)} %concatenate.64.scal, bf16[16,24,1664]{2,1,0:T(8,128)(2,1)} %copy-done.2, ...), custom_call_target="tpu_custom_call" | custom-call | flops 3623878656 | bytes 20000000 | tf_op jit(solution)/shard_map/loss_and_feed_back/pallas_call | solution.py:679
  148.2 20.3 %attention_back.1 = (bf16[768,1536]{1,0:T(8,128)(2,1)}, bf16[768,1536]{1,0:T(8,128)(2,1)}, f32[24,8,768]{2,1,0:T(8,128)}, bf16[24,8,768]{2,1,0:T(8,128)(2,1)}, f32[8,768]{1,0:T(8,128)}) custom-call(s32[36]{0:T(128)} %concatenate.64.scal, f32[384,768]{1,0:T(8,128)} %get-tuple-element.39.dm, bf16[768,768]{1,0:T(8,128)(2,1)} %bitcast.63, bf16[2,768]{1,0:T(2,128)(2,1)} %gains.7, ...), custom_call_target="tpu_custom_call" | custom-call | flops 3623878656 | bytes 20000000 | tf_op jit(solution)/shard_map/attention_back/pallas_call | solution.py:679
  171.3 1.2 slice.217
  172.4 1.2 slice.218
  177.1 1.1 pad_maximum_fusion.1
  180.2 1.3 collective-permute-start.18
  182.0 1.8 collective-permute-start.20
  183.8 2.4 convert_add_fusion.1
  186.8 1.3 collective-permute-start.11
  188.8 7.7 %collective-permute-done.18 = bf16[192,1536]{1,0:T(8,128)(2,1)S(1)} collective-permute-done((bf16[192,1536]{1,0:T(8,128)(2,1)S(1)}, bf16[192,1536]{1,0:T(8,128)(2,1)S(1)}, u32[]{:S(2)}, u32[]{:S(2)}) %collective-permute-start.18) | collective-permute-done | bytes 589856 | tf_op jit(solution)/shard_map/ppermute | solution.py:620
  196.5 1.2 collective-permute-start.13
  197.6 12.8 %collective-permute-done.19 = bf16[192,1536]{1,0:T(8,128)(2,1)S(1)} collective-permute-done((bf16[192,1536]{1,0:T(8,128)(2,1)S(1)}, bf16[192,1536]{1,0:T(8,128)(2,1)S(1)}, u32[]{:S(2)}, u32[]{:S(2)}) %collective-permute-start.19) | collective-permute-done | bytes 589856 | tf_op jit(solution)/shard_map/ppermute | solution.py:620
  211.4 1.3 collective-permute-start.22
  212.8 10.1 %collective-permute-done.11 = bf16[192,1664]{1,0:T(8,128)(2,1)S(1)} collective-permute-done((bf16[192,1664]{1,0:T(8,128)(2,1)S(1)}, bf16[192,1664]{1,0:T(8,128)(2,1)S(1)}, u32[]{:S(2)}, u32[]{:S(2)}) %collective-permute-start.11) | collective-permute-done | bytes 639008 | tf_op jit(solution)/shard_map/ppermute | solution.py:620
  222.8 2.0 collective-permute-start.23
  225.0 11.7 %collective-permute-done.12 = bf16[192,1664]{1,0:T(8,128)(2,1)S(1)} collective-permute-done((bf16[192,1664]{1,0:T(8,128)(2,1)S(1)}, bf16[192,1664]{1,0:T(8,128)(2,1)S(1)}, u32[]{:S(2)}, u32[]{:S(2)}) %collective-permute-start.12) | collective-permute-done | bytes 639008 | tf_op jit(solution)/shard_map/ppermute | solution.py:620
  240.1 2.7 %collective-permute-start.14 = (bf16[48,1664]{1,0:T(8,128)(2,1)S(1)}, bf16[48,1664]{1,0:T(8,128)(2,1)S(1)}, u32[]{:S(2)}, u32[]{:S(2)}) collective-permute-start(bf16[48,1664]{1,0:T(8,128)(2,1)S(1)} %pad_maximum_fusion.7), channel_id=1, source_target_pairs={{0,4},{1,5},{2,6},{3,7},{4,0},{5,1},{6,2},{7,3},{8,12},{9,13},{10,... | collective-permute-start | bytes 479240 | tf_op jit(solution)/shard_map/ppermute | solution.py:620
  243.6 3.5 %collective-permute-done.16 = bf16[48,1664]{1,0:T(8,128)(2,1)S(1)} collective-permute-done((bf16[48,1664]{1,0:T(8,128)(2,1)S(1)}, bf16[48,1664]{1,0:T(8,128)(2,1)S(1)}, u32[]{:S(2)}, u32[]{:S(2)}) %collective-permute-start.16) | collective-permute-done | bytes 159776 | tf_op jit(solution)/shard_map/ppermute | solution.py:620
  247.2 6.3 %collective-permute-done.15 = bf16[48,1664]{1,0:T(8,128)(2,1)S(1)} collective-permute-done((bf16[48,1664]{1,0:T(8,128)(2,1)S(1)}, bf16[48,1664]{1,0:T(8,128)(2,1)S(1)}, u32[]{:S(2)}, u32[]{:S(2)}) %collective-permute-start.15) | collective-permute-done | bytes 159776 | tf_op jit(solution)/shard_map/ppermute | solution.py:620
  (131 shorter events, 27.9 us)
Async XLA Ops:
  2.6 5.3 %copy-start.7 = (bf16[3072]{0:T(1024)(128)(2,1)S(1)}, bf16[3072]{0:T(1024)(128)(2,1)}, u32[]{:S(2)}) copy-start(bf16[3072]{0:T(1024)(128)(2,1)} %param.27) | copy-start | bytes 18436
  67.4 6.6 %collective-permute-start = (bf16[1,24,1664]{2,1,0:T(8,128)(2,1)}, bf16[1,24,1664]{2,1,0:T(8,128)(2,1)S(1)}, u32[]{:S(2)}, u32[]{:S(2)}) collective-permute-start(bf16[1,24,1664]{2,1,0:T(8,128)(2,1)} %bitcast.67), channel_id=1, source_target_pairs={{0,4},{1,5},{2,6},{3,7},{4,0},{5,1},{6,2},{7,3},{8,12},{9,13},{10,... | collective-permute-start | bytes 239624 | tf_op jit(solution)/shard_map/ppermute | solution.py:620
  70.5 9.2 %collective-permute-start.1 = (bf16[1,24,1664]{2,1,0:T(8,128)(2,1)}, bf16[1,24,1664]{2,1,0:T(8,128)(2,1)S(1)}, u32[]{:S(2)}, u32[]{:S(2)}) collective-permute-start(bf16[1,24,1664]{2,1,0:T(8,128)(2,1)} %bitcast.68), channel_id=1, source_target_pairs={{0,8},{1,9},{2,10},{3,11},{4,12},{5,13},{6,14},{7,15},{8,0},{9,1},... | collective-permute-start | bytes 239624 | tf_op jit(solution)/shard_map/ppermute | solution.py:620
  73.1 6.7 %collective-permute-start.2 = (bf16[1,24,1664]{2,1,0:T(8,128)(2,1)}, bf16[1,24,1664]{2,1,0:T(8,128)(2,1)S(1)}, u32[]{:S(2)}, u32[]{:S(2)}) collective-permute-start(bf16[1,24,1664]{2,1,0:T(8,128)(2,1)} %bitcast.69), channel_id=1, source_target_pairs={{0,12},{1,13},{2,14},{3,15},{4,8},{5,9},{6,10},{7,11},{8,4},{9,5},... | collective-permute-start | bytes 239624 | tf_op jit(solution)/shard_map/ppermute | solution.py:620
  80.7 15.7 %copy-start.5 = (bf16[24,3072]{1,0:T(8,128)(2,1)S(1)}, bf16[24,3072]{1,0:T(8,128)(2,1)}, u32[]{:S(2)}) copy-start(bf16[24,3072]{1,0:T(8,128)(2,1)} %get-tuple-element.33) | copy-start | bytes 442372
  80.7 10.5 %collective-permute-start.3 = (bf16[4,24,1664]{2,1,0:T(8,128)(2,1)S(1)}, bf16[4,24,1664]{2,1,0:T(8,128)(2,1)S(1)}, u32[]{:S(2)}, u32[]{:S(2)}) collective-permute-start(bf16[4,24,1664]{2,1,0:T(8,128)(2,1)S(1)} %pad_maximum_fusion.5), channel_id=1, source_target_pairs={{0,1},{1,0},{2,3},{3,2},{4,5},{5,4},{6,7},{7,6},{8,9},{9,8},{10,11... | collective-permute-start | bytes 958472 | tf_op jit(solution)/shard_map/ppermute | solution.py:620
  82.2 13.9 %collective-permute-start.4 = (bf16[4,24,1664]{2,1,0:T(8,128)(2,1)S(1)}, bf16[4,24,1664]{2,1,0:T(8,128)(2,1)S(1)}, u32[]{:S(2)}, u32[]{:S(2)}) collective-permute-start(bf16[4,24,1664]{2,1,0:T(8,128)(2,1)S(1)} %pad_maximum_fusion.5), channel_id=1, source_target_pairs={{0,2},{1,3},{2,0},{3,1},{4,6},{5,7},{6,4},{7,5},{8,10},{9,11},{10,... | collective-permute-start | bytes 958472 | tf_op jit(solution)/shard_map/ppermute | solution.py:620
  83.7 12.5 %collective-permute-start.5 = (bf16[4,24,1664]{2,1,0:T(8,128)(2,1)S(1)}, bf16[4,24,1664]{2,1,0:T(8,128)(2,1)S(1)}, u32[]{:S(2)}, u32[]{:S(2)}) collective-permute-start(bf16[4,24,1664]{2,1,0:T(8,128)(2,1)S(1)} %pad_maximum_fusion.5), channel_id=1, source_target_pairs={{0,3},{1,2},{2,1},{3,0},{4,7},{5,6},{6,5},{7,4},{8,11},{9,10},{10,... | collective-permute-start | bytes 958472 | tf_op jit(solution)/shard_map/ppermute | solution.py:620
  96.3 17.6 %copy-start.2 = (bf16[16,24,1664]{2,1,0:T(8,128)(2,1)}, bf16[16,24,1664]{2,1,0:T(8,128)(2,1)S(1)}, u32[]{:S(2)}) copy-start(bf16[16,24,1664]{2,1,0:T(8,128)(2,1)S(1)} %constant_dynamic-update-slice_fusion.own_any) | copy-start | bytes 3833860
  96.3 17.6 %collective-permute-start.6 = (bf16[16,24,1664]{2,1,0:T(8,128)(2,1)S(1)}, bf16[16,24,1664]{2,1,0:T(8,128)(2,1)S(1)}, u32[]{:S(2)}, u32[]{:S(2)}) collective-permute-start(bf16[16,24,1664]{2,1,0:T(8,128)(2,1)S(1)} %constant_dynamic-update-slice_fusion.own_any), channel_id=1, source_target_pairs={{0,16},{16,0},{1,17},{17,1},{2,18},{18,2},{3,19},{19,3},{4,20},{20... | collective-permute-start | bytes 3833864 | tf_op jit(solution)/shard_map/ppermute | solution.py:620
  97.4 14.4 %all-to-all-start = ((bf16[16,24,2,96]{3,1,2,0:T(8,128)(2,1)}), bf16[16,24,2,96]{3,1,2,0:T(8,128)(2,1)S(1)}, u32[]{:S(2)}, u32[]{:S(2)}) async-start(bf16[16,24,2,96]{3,1,2,0:T(8,128)(2,1)} %bitcast.55), calls=%async_computation | async-start | bytes 393216 | tf_op jit(solution)/shard_map/all_to_all | solution.py:735
  111.8 1.4 collective-permute-start.7
  147.1 31.1 %collective-permute-start.17 = (bf16[768,1536]{1,0:T(8,128)(2,1)}, bf16[768,1536]{1,0:T(8,128)(2,1)S(1)}, u32[]{:S(2)}, u32[]{:S(2)}) collective-permute-start(bf16[768,1536]{1,0:T(8,128)(2,1)} %get-tuple-element.50), channel_id=1, source_target_pairs={{0,16},{16,0},{1,17},{17,1},{2,18},{18,2},{3,19},{19,3},{4,20},{20... | collective-permute-start | bytes 7077896 | tf_op jit(solution)/shard_map/ppermute | solution.py:620
  148.2 21.9 %copy-start.6 = (f32[8,768]{1,0:T(8,128)S(1)}, f32[8,768]{1,0:T(8,128)}, u32[]{:S(2)}) copy-start(f32[8,768]{1,0:T(8,128)} %get-tuple-element.48) | copy-start | bytes 73732
  148.2 22.4 %copy-start.8 = (s32[16]{0:T(128)S(1)}, s32[16]{0:T(128)}, u32[]{:S(2)}) copy-start(s32[16]{0:T(128)} %constant.43) | copy-start | bytes 196
  170.2 3.4 %collective-permute-start.10 = (f32[6,768]{1,0:T(8,128)S(1)}, f32[6,768]{1,0:T(8,128)S(1)}, u32[]{:S(2)}, u32[]{:S(2)}) collective-permute-start(f32[6,768]{1,0:T(8,128)S(1)} %fusion.13), channel_id=1, source_target_pairs={{0,16},{16,0},{1,17},{17,1},{2,18},{18,2},{3,19},{19,3},{4,20},{20... | collective-permute-start | bytes 55304 | tf_op jit(solution)/shard_map/ppermute | solution.py:620
  170.7 13.1 %collective-permute-start.9 = (bf16[768,1536]{1,0:T(8,128)(2,1)}, bf16[768,1536]{1,0:T(8,128)(2,1)}, u32[]{:S(2)}, u32[]{:S(2)}) collective-permute-start(bf16[768,1536]{1,0:T(8,128)(2,1)} %get-tuple-element.46), channel_id=1, source_target_pairs={{0,16},{16,0},{1,17},{17,1},{2,18},{18,2},{3,19},{19,3},{4,20},{20... | collective-permute-start | bytes 7077896 | tf_op jit(solution)/shard_map/ppermute | solution.py:620
  170.9 5.1 %collective-permute-start.8 = (bf16[24,8,768]{2,1,0:T(8,128)(2,1)}, bf16[24,8,768]{2,1,0:T(8,128)(2,1)}, u32[]{:S(2)}, u32[]{:S(2)}) collective-permute-start(bf16[24,8,768]{2,1,0:T(8,128)(2,1)} %get-tuple-element.44), channel_id=1, source_target_pairs={{0,16},{16,0},{1,17},{17,1},{2,18},{18,2},{3,19},{19,3},{4,20},{20... | collective-permute-start | bytes 884744 | tf_op jit(solution)/shard_map/ppermute | solution.py:620
  177.1 2.1 copy-start
  180.1 3.7 %copy-start.1 = (bf16[768,1536]{1,0:T(8,128)(2,1)S(1)}, bf16[768,1536]{1,0:T(8,128)(2,1)}, u32[]{:S(2)}) copy-start(bf16[768,1536]{1,0:T(8,128)(2,1)} %get-tuple-element.45) | copy-start | bytes 7077892
  180.2 16.2 %collective-permute-start.18 = (bf16[192,1536]{1,0:T(8,128)(2,1)S(1)}, bf16[192,1536]{1,0:T(8,128)(2,1)S(1)}, u32[]{:S(2)}, u32[]{:S(2)}) collective-permute-start(bf16[192,1536]{1,0:T(8,128)(2,1)S(1)} %get-tuple-element.65), channel_id=1, source_target_pairs={{0,1},{1,0},{2,3},{3,2},{4,5},{5,4},{6,7},{7,6},{8,9},{9,8},{10,11... | collective-permute-start | bytes 1769480 | tf_op jit(solution)/shard_map/ppermute | solution.py:620
  181.6 28.9 %collective-permute-start.19 = (bf16[192,1536]{1,0:T(8,128)(2,1)S(1)}, bf16[192,1536]{1,0:T(8,128)(2,1)S(1)}, u32[]{:S(2)}, u32[]{:S(2)}) collective-permute-start(bf16[192,1536]{1,0:T(8,128)(2,1)S(1)} %get-tuple-element.67), channel_id=1, source_target_pairs={{0,2},{1,3},{2,0},{3,1},{4,6},{5,7},{6,4},{7,5},{8,10},{9,11},{10,... | collective-permute-start | bytes 1769480 | tf_op jit(solution)/shard_map/ppermute | solution.py:620
  182.0 28.4 %collective-permute-start.20 = (bf16[192,1536]{1,0:T(8,128)(2,1)S(1)}, bf16[192,1536]{1,0:T(8,128)(2,1)S(1)}, u32[]{:S(2)}, u32[]{:S(2)}) collective-permute-start(bf16[192,1536]{1,0:T(8,128)(2,1)S(1)} %get-tuple-element.66), channel_id=1, source_target_pairs={{0,3},{1,2},{2,1},{3,0},{4,7},{5,6},{6,5},{7,4},{8,11},{9,10},{10,... | collective-permute-start | bytes 1769480 | tf_op jit(solution)/shard_map/ppermute | solution.py:620
  186.8 36.1 %collective-permute-start.11 = (bf16[192,1664]{1,0:T(8,128)(2,1)S(1)}, bf16[192,1664]{1,0:T(8,128)(2,1)S(1)}, u32[]{:S(2)}, u32[]{:S(2)}) collective-permute-start(bf16[192,1664]{1,0:T(8,128)(2,1)S(1)} %pad_maximum_fusion.2), channel_id=1, source_target_pairs={{0,1},{1,0},{2,3},{3,2},{4,5},{5,4},{6,7},{7,6},{8,9},{9,8},{10,11... | collective-permute-start | bytes 1916936 | tf_op jit(solution)/shard_map/ppermute | solution.py:620
  188.2 48.5 %collective-permute-start.12 = (bf16[192,1664]{1,0:T(8,128)(2,1)S(1)}, bf16[192,1664]{1,0:T(8,128)(2,1)S(1)}, u32[]{:S(2)}, u32[]{:S(2)}) collective-permute-start(bf16[192,1664]{1,0:T(8,128)(2,1)S(1)} %pad_maximum_fusion.3), channel_id=1, source_target_pairs={{0,2},{1,3},{2,0},{3,1},{4,6},{5,7},{6,4},{7,5},{8,10},{9,11},{10,... | collective-permute-start | bytes 1916936 | tf_op jit(solution)/shard_map/ppermute | solution.py:620
  196.5 40.5 %collective-permute-start.13 = (bf16[192,1664]{1,0:T(8,128)(2,1)S(1)}, bf16[192,1664]{1,0:T(8,128)(2,1)S(1)}, u32[]{:S(2)}, u32[]{:S(2)}) collective-permute-start(bf16[192,1664]{1,0:T(8,128)(2,1)S(1)} %pad_maximum_fusion.4), channel_id=1, source_target_pairs={{0,3},{1,2},{2,1},{3,0},{4,7},{5,6},{6,5},{7,4},{8,11},{9,10},{10,... | collective-permute-start | bytes 1916936 | tf_op jit(solution)/shard_map/ppermute | solution.py:620
  210.8 29.3 %collective-permute-start.21 = (bf16[48,1536]{1,0:T(8,128)(2,1)S(1)}, bf16[48,1536]{1,0:T(8,128)(2,1)S(1)}, u32[]{:S(2)}, u32[]{:S(2)}) collective-permute-start(bf16[48,1536]{1,0:T(8,128)(2,1)S(1)} %get-tuple-element.76), channel_id=1, source_target_pairs={{0,4},{1,5},{2,6},{3,7},{4,0},{5,1},{6,2},{7,3},{8,12},{9,13},{10,... | collective-permute-start | bytes 442376 | tf_op jit(solution)/shard_map/ppermute | solution.py:620
  211.4 31.4 %collective-permute-start.22 = (bf16[48,1536]{1,0:T(8,128)(2,1)S(1)}, bf16[48,1536]{1,0:T(8,128)(2,1)S(1)}, u32[]{:S(2)}, u32[]{:S(2)}) collective-permute-start(bf16[48,1536]{1,0:T(8,128)(2,1)S(1)} %get-tuple-element.78), channel_id=1, source_target_pairs={{0,8},{1,9},{2,10},{3,11},{4,12},{5,13},{6,14},{7,15},{8,0},{9,1},... | collective-permute-start | bytes 442376 | tf_op jit(solution)/shard_map/ppermute | solution.py:620
  222.8 20.0 %collective-permute-start.23 = (bf16[48,1536]{1,0:T(8,128)(2,1)S(1)}, bf16[48,1536]{1,0:T(8,128)(2,1)S(1)}, u32[]{:S(2)}, u32[]{:S(2)}) collective-permute-start(bf16[48,1536]{1,0:T(8,128)(2,1)S(1)} %get-tuple-element.77), channel_id=1, source_target_pairs={{0,12},{1,13},{2,14},{3,15},{4,8},{5,9},{6,10},{7,11},{8,4},{9,5},... | collective-permute-start | bytes 442376 | tf_op jit(solution)/shard_map/ppermute | solution.py:620
  238.2 8.9 %collective-permute-start.16 = (bf16[48,1664]{1,0:T(8,128)(2,1)S(1)}, bf16[48,1664]{1,0:T(8,128)(2,1)S(1)}, u32[]{:S(2)}, u32[]{:S(2)}) collective-permute-start(bf16[48,1664]{1,0:T(8,128)(2,1)S(1)} %pad_maximum_fusion.9), channel_id=1, source_target_pairs={{0,12},{1,13},{2,14},{3,15},{4,8},{5,9},{6,10},{7,11},{8,4},{9,5},... | collective-permute-start | bytes 479240 | tf_op jit(solution)/shard_map/ppermute | solution.py:620
  239.4 14.1 %collective-permute-start.15 = (bf16[48,1664]{1,0:T(8,128)(2,1)S(1)}, bf16[48,1664]{1,0:T(8,128)(2,1)S(1)}, u32[]{:S(2)}, u32[]{:S(2)}) collective-permute-start(bf16[48,1664]{1,0:T(8,128)(2,1)S(1)} %pad_maximum_fusion.8), channel_id=1, source_target_pairs={{0,8},{1,9},{2,10},{3,11},{4,12},{5,13},{6,14},{7,15},{8,0},{9,1},... | collective-permute-start | bytes 479240 | tf_op jit(solution)/shard_map/ppermute | solution.py:620
  240.1 13.5 %collective-permute-start.14 = (bf16[48,1664]{1,0:T(8,128)(2,1)S(1)}, bf16[48,1664]{1,0:T(8,128)(2,1)S(1)}, u32[]{:S(2)}, u32[]{:S(2)}) collective-permute-start(bf16[48,1664]{1,0:T(8,128)(2,1)S(1)} %pad_maximum_fusion.7), channel_id=1, source_target_pairs={{0,4},{1,5},{2,6},{3,7},{4,0},{5,1},{6,2},{7,3},{8,12},{9,13},{10,... | collective-permute-start | bytes 479240 | tf_op jit(solution)/shard_map/ppermute | solution.py:620
  (2 other events, 3.0 us)
